TPU v7x, 256 devices: a whole 4x4x8 slice. The times are simulated.
256 devices in a mesh: dp: 8 (over y, core), ctx: 32 (over x, z).
Axes of the slice: x: 4, y: 4, z: 8, core: 2. Of those that a mesh axis runs over, the one named last changes fastest.
Arguments:
- queries: bfloat16 [131072, 256], P(('dp', 'ctx')), parts along dimension 0, may hold values from -90 to 90
- keys: bfloat16 [131072, 128], P(('dp', 'ctx')), parts along dimension 0, may hold values from -4.5 to 4.5
- values: bfloat16 [131072, 128], P(('dp', 'ctx')), parts along dimension 0, may hold values from -6 to 6
- cotangent: bfloat16 [131072, 256], P(('dp', 'ctx')), parts along dimension 0, may hold values from -6 to 6
- doc_lengths: int32 [512], P('dp'), parts along dimension 0, may hold values from 1 to 1024, 16384 in all
- old_slots: int32 [4096], P('dp'), parts along dimension 0, may hold values from 0 to 511, as said below
Outputs:
- attended: bfloat16 [131072, 256], P(('dp', 'ctx')), parts along dimension 0
- query_grad: float32 [131072, 256], P(('dp', 'ctx')), parts along dimension 0
- key_grad: float32 [131072, 128], P(('dp', 'ctx')), parts along dimension 0
- value_grad: float32 [131072, 128], P(('dp', 'ctx')), parts along dimension 0
There are 8 independent parts, one for each index of `dp`. A program takes and returns all parts, laid end to end along the dimension named above; each array names one. Nothing has to cross between parts.
Inputs may be any that keep to these rules, and one draw needn't show every extreme that they name: `old_slots`: each old slot appears once. Old slot s lies on device s // 16 and block b on device b // 16. The 16 old slots of one device hold blocks of 16 different devices when 16 is at most the number of devices, else the same number of blocks of every device. `doc_lengths`: the lengths sum to 16384.
All inputs are finite; a program needn't handle non-finite values.
Results may differ from a plain program's by a relative error of at most 0.035.
Values may be sent and summed in bfloat16 or wider, within the bound.
A program may use at most 64 MiB of HBM per device.

v0:
```python
from functools import partial

import jax
import jax.numpy as jnp
from jax import lax
from jax.sharding import PartitionSpec as P

ROWS_BLK = 32
REACH = 2


NEGATIVE = -1e30


def from_behind(value, axis, steps):
    count = lax.axis_size(axis)
    first, last = (max(0, -steps), min(count, count - steps))
    return lax.ppermute(value, axis, [(source, source + steps) for source in range(first, last)])


def doc_index(positions, doc_ends):
    return jnp.sum((doc_ends[None, :] <= positions[:, None]).astype(jnp.int32), axis=1)


def allowed_mask(query_pos, query_doc, key_pos, key_doc):
    same_doc = query_doc[:, None] == key_doc[None, :]
    causal = key_pos[None, :] <= query_pos[:, None]
    return same_doc & causal & (key_pos[None, :] >= 0)


def contract_rows(left, right):
    return lax.dot_general(
        left, right, (((0,), (0,)), ((), ())), preferred_element_type=jnp.float32
    )


def head_scores(query_head, key_block, allowed, factor):
    raw = (
        lax.dot_general(
            query_head, key_block, (((1,), (1,)), ((), ())), preferred_element_type=jnp.float32
        )
        * factor
    )
    return jnp.where(allowed, raw, NEGATIVE)


def piece_stats(query_head, allowed, key_block, factor):
    scores = head_scores(query_head, key_block, allowed, factor)
    peak = jnp.max(scores, axis=1)
    return (peak, jnp.sum(jnp.exp(scores - peak[:, None]), axis=1))


def piece_output(query_head, allowed, key_block, value_block, lse_head, factor):
    scores = head_scores(query_head, key_block, allowed, factor)
    weights_low = jnp.exp(scores - lse_head[:, None]).astype(jnp.bfloat16)
    return jnp.dot(weights_low, value_block, preferred_element_type=jnp.float32)


def tile_terms(
    query_head, grad_head, lse_head, delta_head, allowed, key_block, value_block, factor
):
    scores = head_scores(query_head, key_block, allowed, factor)
    weights = jnp.exp(scores - lse_head[:, None])
    grad_weights = lax.dot_general(
        grad_head, value_block, (((1,), (1,)), ((), ())), preferred_element_type=jnp.float32
    )
    grad_scores = (weights * (grad_weights - delta_head[:, None])).astype(jnp.bfloat16)
    return (weights.astype(jnp.bfloat16), grad_scores)


def query_side(
    query_head, grad_head, lse_head, delta_head, allowed, key_block, value_block, factor
):
    weights_low, grad_scores = tile_terms(
        query_head, grad_head, lse_head, delta_head, allowed, key_block, value_block, factor
    )
    return jnp.dot(grad_scores, key_block, preferred_element_type=jnp.float32)


def key_side(query_head, grad_head, lse_head, delta_head, allowed, key_block, value_block, factor):
    weights_low, grad_scores = tile_terms(
        query_head, grad_head, lse_head, delta_head, allowed, key_block, value_block, factor
    )
    return (contract_rows(grad_scores, query_head), contract_rows(weights_low, grad_head))


def full_side(query_head, grad_head, lse_head, delta_head, allowed, key_block, value_block, factor):
    weights_low, grad_scores = tile_terms(
        query_head, grad_head, lse_head, delta_head, allowed, key_block, value_block, factor
    )
    query_term = jnp.dot(grad_scores, key_block, preferred_element_type=jnp.float32)
    return (
        query_term,
        contract_rows(grad_scores, query_head),
        contract_rows(weights_low, grad_head),
    )


def select_blocks(table, array, have_blocks, give_blocks):
    block_rows = array.shape[0] // have_blocks
    flat_blocks = array.reshape(have_blocks, block_rows * array.shape[1])
    picked = jnp.dot(table, flat_blocks, preferred_element_type=jnp.float32).astype(jnp.bfloat16)
    return picked.reshape(give_blocks * block_rows, array.shape[1])


def on_device(queries, keys, values, cotangent, doc_lengths, old_slots):
    row_count = queries.shape[0]
    head_dim = keys.shape[1]
    head_count = queries.shape[1] // head_dim
    per_dev = row_count // ROWS_BLK
    members = lax.axis_size("ctx")
    own_index = lax.axis_index("ctx")
    per_peer = max(1, per_dev // members)
    factor = head_dim ** (-0.5)
    slot_ids = jnp.arange(members * per_peer, dtype=jnp.int32)
    held_ids = jnp.arange(per_dev, dtype=jnp.int32)
    held_slots = own_index * per_dev + held_ids
    every_block = jnp.arange(old_slots.shape[0], dtype=jnp.int32)
    logical = jnp.sum(
        jnp.where(old_slots[None, :] == held_slots[:, None], every_block[None, :], 0), axis=1
    )
    dest_dev = logical // per_dev
    earlier = (held_ids[None, :] < held_ids[:, None]) & (dest_dev[None, :] == dest_dev[:, None])
    send_rank = jnp.sum(earlier.astype(jnp.int32), axis=1)
    send_table = (slot_ids[:, None] == (dest_dev * per_peer + send_rank)[None, :]).astype(
        jnp.bfloat16
    )
    wanted = lax.dynamic_slice_in_dim(old_slots, own_index * per_dev, per_dev)
    source_dev = wanted // per_dev
    before = (wanted[None, :] < wanted[:, None]) & (source_dev[None, :] == source_dev[:, None])
    recv_rank = jnp.sum(before.astype(jnp.int32), axis=1)
    recv_table = ((source_dev * per_peer + recv_rank)[:, None] == slot_ids[None, :]).astype(
        jnp.bfloat16
    )
    query_out = select_blocks(send_table, queries, per_dev, members * per_peer)
    key_out = select_blocks(send_table, keys, per_dev, members * per_peer)
    value_out = select_blocks(send_table, values, per_dev, members * per_peer)
    query_in, key_in, value_in = (
        lax.all_to_all(query_out, "ctx", split_axis=0, concat_axis=0, tiled=True),
        lax.all_to_all(key_out, "ctx", split_axis=0, concat_axis=0, tiled=True),
        lax.all_to_all(value_out, "ctx", split_axis=0, concat_axis=0, tiled=True),
    )
    query_new = select_blocks(recv_table, query_in, members * per_peer, per_dev)
    key_new = select_blocks(recv_table, key_in, members * per_peer, per_dev)
    value_new = select_blocks(recv_table, value_in, members * per_peer, per_dev)
    doc_ends = jnp.cumsum(doc_lengths)
    own_pos = own_index * row_count + jnp.arange(row_count, dtype=jnp.int32)
    own_doc = doc_index(own_pos, doc_ends)
    pieces = [(key_new, value_new, own_pos, own_doc)]
    for distance in range(1, REACH + 1):
        key_far, value_far = from_behind((key_new, value_new), "ctx", distance)
        far_pos = own_pos - distance * row_count
        pieces.append((key_far, value_far, far_pos, doc_index(far_pos, doc_ends)))
    masks = [allowed_mask(own_pos, own_doc, piece[2], piece[3]) for piece in pieces]
    zero_rows = jnp.zeros((row_count,), jnp.float32)
    zero_block = jnp.zeros((row_count, head_dim), jnp.float32)
    lse_list = []
    out_list = []
    for head_id in range(head_count):
        query_head = query_new[:, head_id * head_dim : (head_id + 1) * head_dim]
        running_max = jnp.full((row_count,), NEGATIVE, jnp.float32)
        running_sum = zero_rows
        for piece_id in range(len(pieces)):
            compute = partial(piece_stats, query_head, masks[piece_id], pieces[piece_id][0], factor)
            if piece_id == 0:
                peak, piece_sum = compute()
            else:
                peak, piece_sum = compute()
            new_max = jnp.maximum(running_max, peak)
            running_sum = running_sum * jnp.exp(running_max - new_max) + piece_sum * jnp.exp(
                peak - new_max
            )
            running_max = new_max
        lse_head = running_max + jnp.log(running_sum)
        accum = zero_block
        for piece_id in range(len(pieces)):
            compute = partial(
                piece_output,
                query_head,
                masks[piece_id],
                pieces[piece_id][0],
                pieces[piece_id][1],
                lse_head,
                factor,
            )
            if piece_id == 0:
                accum = compute()
            else:
                accum = accum + compute()
        lse_list.append(lse_head)
        out_list.append(accum.astype(jnp.bfloat16))
    attended = jnp.concatenate(out_list, axis=1)
    lse_all = jnp.stack(lse_list)
    grad_heads = [
        cotangent[:, head_id * head_dim : (head_id + 1) * head_dim] for head_id in range(head_count)
    ]
    delta_all = jnp.stack(
        [
            jnp.sum(
                grad_heads[head_id].astype(jnp.float32) * out_list[head_id].astype(jnp.float32),
                axis=1,
            )
            for head_id in range(head_count)
        ]
    )
    query_terms = [zero_block for head_id in range(head_count)]
    key_grad = zero_block
    value_grad = zero_block
    for head_id in range(head_count):
        query_head = query_new[:, head_id * head_dim : (head_id + 1) * head_dim]
        own_terms = full_side(
            query_head,
            grad_heads[head_id],
            lse_all[head_id],
            delta_all[head_id],
            masks[0],
            key_new,
            value_new,
            factor,
        )
        query_terms[head_id] = own_terms[0]
        key_grad = key_grad + own_terms[1]
        value_grad = value_grad + own_terms[2]
        for piece_id in range(1, len(pieces)):
            compute = partial(
                query_side,
                query_head,
                grad_heads[head_id],
                lse_all[head_id],
                delta_all[head_id],
                masks[piece_id],
                pieces[piece_id][0],
                pieces[piece_id][1],
                factor,
            )
            query_terms[head_id] = query_terms[head_id] + compute()
    for distance in range(1, REACH + 1):
        query_near, grad_near = from_behind((query_new, cotangent), "ctx", -distance)
        lse_near, delta_near = from_behind((lse_all, delta_all), "ctx", -distance)
        near_pos = own_pos + distance * row_count
        near_doc = doc_index(near_pos, doc_ends)
        near_allowed = allowed_mask(near_pos, near_doc, own_pos, own_doc)
        for head_id in range(head_count):
            columns = slice(head_id * head_dim, (head_id + 1) * head_dim)
            compute = partial(
                key_side,
                query_near[:, columns],
                grad_near[:, columns],
                lse_near[head_id],
                delta_near[head_id],
                near_allowed,
                key_new,
                value_new,
                factor,
            )
            key_term, value_term = compute()
            key_grad = key_grad + key_term
            value_grad = value_grad + value_term
    query_grad = jnp.concatenate(query_terms, axis=1) * factor
    return (attended, query_grad, key_grad * factor, value_grad)


def solution(mesh):
    return jax.shard_map(
        on_device,
        mesh=mesh,
        in_specs=(
            P(("dp", "ctx"), None),
            P(("dp", "ctx"), None),
            P(("dp", "ctx"), None),
            P(("dp", "ctx"), None),
            P("dp"),
            P("dp"),
        ),
        out_specs=(
            P(("dp", "ctx"), None),
            P(("dp", "ctx"), None),
            P(("dp", "ctx"), None),
            P(("dp", "ctx"), None),
        ),
        check_vma=False,
    )
```

profile of v0, /device:TPU:10, one launch (start us, length us, event | category | flops | bytes accessed | tf_op | source)
XLA Modules:
  0.0 176.4 jit_solution(8011702866726478793)
XLA Ops:
  0.6 8.2 %collective-permute-start.10 = (bf16[512,256]{1,0:T(8,128)(2,1)}, bf16[512,256]{1,0:T(8,128)(2,1)}, u32[]{:S(2)}, u32[]{:S(2)}) collective-permute-start(bf16[512,256]{1,0:T(8,128)(2,1)} %param.9), channel_id=1, source_target_pairs={{2,0},{3,1},{4,2},{5,3},{6,4},{7,5},{8,6},{9,7},{10,8},{11,9},{12,... | collective-permute-start | bytes 786440 | tf_op jit(solution)/shard_map/ppermute | solution.py:18
  8.8 2.9 %collective-permute-start.6 = (bf16[512,256]{1,0:T(8,128)(2,1)}, bf16[512,256]{1,0:T(8,128)(2,1)}, u32[]{:S(2)}, u32[]{:S(2)}) collective-permute-start(bf16[512,256]{1,0:T(8,128)(2,1)} %param.9), channel_id=1, source_target_pairs={{1,0},{2,1},{3,2},{4,3},{5,4},{6,5},{7,6},{8,7},{9,8},{10,9},{11,1... | collective-permute-start | bytes 786440 | tf_op jit(solution)/shard_map/ppermute | solution.py:18
  14.8 6.7 %all-to-all-start.1 = ((bf16[32,32,128]{2,1,0:T(8,128)(2,1)}), bf16[32,32,128]{2,1,0:T(8,128)(2,1)S(1)}, u32[]{:S(2)}, u32[]{:S(2)}) async-start(bf16[32,32,128]{2,1,0:T(8,128)(2,1)} %bitcast.38), calls=%async_computation.1 | async-start | bytes 524288 | tf_op jit(solution)/shard_map/all_to_all | solution.py:140
  24.1 8.4 %all-to-all-done.1 = bf16[32,32,128]{2,1,0:T(8,128)(2,1)S(1)} async-done(((bf16[32,32,128]{2,1,0:T(8,128)(2,1)}), bf16[32,32,128]{2,1,0:T(8,128)(2,1)S(1)}, u32[]{:S(2)}, u32[]{:S(2)}) %all-to-all-start.1) | async-done | bytes 262176 | tf_op jit(solution)/shard_map/all_to_all | solution.py:140
  32.5 9.4 %all-to-all-start.2 = ((bf16[32,32,128]{2,1,0:T(8,128)(2,1)}), bf16[32,32,128]{2,1,0:T(8,128)(2,1)S(1)}, u32[]{:S(2)}, u32[]{:S(2)}) async-start(bf16[32,32,128]{2,1,0:T(8,128)(2,1)} %bitcast.42), calls=%async_computation.2 | async-start | bytes 524288 | tf_op jit(solution)/shard_map/all_to_all | solution.py:141
  45.0 7.5 %all-to-all-done.2 = bf16[32,32,128]{2,1,0:T(8,128)(2,1)S(1)} async-done(((bf16[32,32,128]{2,1,0:T(8,128)(2,1)}), bf16[32,32,128]{2,1,0:T(8,128)(2,1)S(1)}, u32[]{:S(2)}, u32[]{:S(2)}) %all-to-all-start.2) | async-done | bytes 262176 | tf_op jit(solution)/shard_map/all_to_all | solution.py:141
  52.4 5.6 %all-to-all-start = ((bf16[32,32,256]{2,1,0:T(8,128)(2,1)}), bf16[32,32,256]{2,1,0:T(8,128)(2,1)S(1)}, u32[]{:S(2)}, u32[]{:S(2)}) async-start(bf16[32,32,256]{2,1,0:T(8,128)(2,1)} %bitcast.34), calls=%async_computation | async-start | bytes 1048576 | tf_op jit(solution)/shard_map/all_to_all | solution.py:139
  59.8 4.3 %collective-permute-start.3 = (bf16[512,128]{1,0:T(8,128)(2,1)S(1)}, bf16[512,128]{1,0:T(8,128)(2,1)S(1)}, u32[]{:S(2)}, u32[]{:S(2)}) collective-permute-start(bf16[512,128]{1,0:T(8,128)(2,1)S(1)} %reshape.473), channel_id=1, source_target_pairs={{0,2},{1,3},{2,4},{3,5},{4,6},{5,7},{6,8},{7,9},{8,10},{9,11},{10,... | collective-permute-start | bytes 393224 | tf_op jit(solution)/shard_map/ppermute | solution.py:18
  64.1 3.4 %collective-permute-start.2 = (bf16[512,128]{1,0:T(8,128)(2,1)S(1)}, bf16[512,128]{1,0:T(8,128)(2,1)S(1)}, u32[]{:S(2)}, u32[]{:S(2)}) collective-permute-start(bf16[512,128]{1,0:T(8,128)(2,1)S(1)} %reshape.473), channel_id=1, source_target_pairs={{0,1},{1,2},{2,3},{3,4},{4,5},{5,6},{6,7},{7,8},{8,9},{9,10},{10,1... | collective-permute-start | bytes 393224 | tf_op jit(solution)/shard_map/ppermute | solution.py:18
  67.8 4.6 %collective-permute-start = (bf16[512,128]{1,0:T(8,128)(2,1)S(1)}, bf16[512,128]{1,0:T(8,128)(2,1)S(1)}, u32[]{:S(2)}, u32[]{:S(2)}) collective-permute-start(bf16[512,128]{1,0:T(8,128)(2,1)S(1)} %reshape.470), channel_id=1, source_target_pairs={{0,1},{1,2},{2,3},{3,4},{4,5},{5,6},{6,7},{7,8},{8,9},{9,10},{10,1... | collective-permute-start | bytes 393224 | tf_op jit(solution)/shard_map/ppermute | solution.py:18
  72.4 3.0 %all-to-all-done = bf16[32,32,256]{2,1,0:T(8,128)(2,1)S(1)} async-done(((bf16[32,32,256]{2,1,0:T(8,128)(2,1)}), bf16[32,32,256]{2,1,0:T(8,128)(2,1)S(1)}, u32[]{:S(2)}, u32[]{:S(2)}) %all-to-all-start) | async-done | bytes 524320 | tf_op jit(solution)/shard_map/all_to_all | solution.py:139
  78.1 4.4 %collective-permute-done = bf16[512,128]{1,0:T(8,128)(2,1)S(1)} collective-permute-done((bf16[512,128]{1,0:T(8,128)(2,1)S(1)}, bf16[512,128]{1,0:T(8,128)(2,1)S(1)}, u32[]{:S(2)}, u32[]{:S(2)}) %collective-permute-start) | collective-permute-done | bytes 131104 | tf_op jit(solution)/shard_map/ppermute | solution.py:18
  82.5 2.1 %collective-permute-start.1 = (bf16[512,128]{1,0:T(8,128)(2,1)S(1)}, bf16[512,128]{1,0:T(8,128)(2,1)S(1)}, u32[]{:S(2)}, u32[]{:S(2)}) collective-permute-start(bf16[512,128]{1,0:T(8,128)(2,1)S(1)} %reshape.470), channel_id=1, source_target_pairs={{0,2},{1,3},{2,4},{3,5},{4,6},{5,7},{6,8},{7,9},{8,10},{9,11},{10,... | collective-permute-start | bytes 393224 | tf_op jit(solution)/shard_map/ppermute | solution.py:18
  86.2 6.9 %collective-permute-done.1 = bf16[512,128]{1,0:T(8,128)(2,1)S(1)} collective-permute-done((bf16[512,128]{1,0:T(8,128)(2,1)S(1)}, bf16[512,128]{1,0:T(8,128)(2,1)S(1)}, u32[]{:S(2)}, u32[]{:S(2)}) %collective-permute-start.1) | collective-permute-done | bytes 131104 | tf_op jit(solution)/shard_map/ppermute | solution.py:18
  93.1 2.6 %collective-permute-start.8 = (bf16[512,256]{1,0:T(8,128)(2,1)}, bf16[512,256]{1,0:T(8,128)(2,1)}, u32[]{:S(2)}, u32[]{:S(2)}) collective-permute-start(bf16[512,256]{1,0:T(8,128)(2,1)} %reshape.467), channel_id=1, source_target_pairs={{2,0},{3,1},{4,2},{5,3},{6,4},{7,5},{8,6},{9,7},{10,8},{11,9},{12,... | collective-permute-start | bytes 786440 | tf_op jit(solution)/shard_map/ppermute | solution.py:18
  98.2 6.0 %collective-permute-start.4 = (bf16[512,256]{1,0:T(8,128)(2,1)}, bf16[512,256]{1,0:T(8,128)(2,1)}, u32[]{:S(2)}, u32[]{:S(2)}) collective-permute-start(bf16[512,256]{1,0:T(8,128)(2,1)} %reshape.467), channel_id=1, source_target_pairs={{1,0},{2,1},{3,2},{4,3},{5,4},{6,5},{7,6},{8,7},{9,8},{10,9},{11,1... | collective-permute-start | bytes 786440 | tf_op jit(solution)/shard_map/ppermute | solution.py:18
  123.5 2.3 %fusion.59 = f32[512,128]{0,1:T(8,128)} fusion(f32[512,128]{0,1:T(8,128)} %fusion.221, bf16[512,128]{1,0:T(8,128)(2,1)} %copy-done.20, bf16[512,128]{1,0:T(8,128)(2,1)} %copy-done.5, f32[512,512]{0,1:T(8,128)S(1)} %get-tuple-element.38, f32[512]{0:T(512)S(1)} %get-tuple-element.45, f32[512]{0:T(512)S(1)} %log_add_fusion.2, bf16[512,256]{1,0:T(8,128)(2,1)S(1)} %copy-done.1), kind=kOutput, calls=%fused_computation.85 | convolution fusion | flops 135331840 | bytes 1970176 | tf_op jit(solution)/shard_map/dot_general | solution.py:77
  133.3 2.4 %collective-permute-start.5 = (f32[2,512]{1,0:T(2,128)}, f32[2,512]{1,0:T(2,128)S(1)}, u32[]{:S(2)}, u32[]{:S(2)}) collective-permute-start(f32[2,512]{1,0:T(2,128)} %pad_maximum_fusion.1), channel_id=1, source_target_pairs={{1,0},{2,1},{3,2},{4,3},{5,4},{6,5},{7,6},{8,7},{9,8},{10,9},{11,1... | collective-permute-start | bytes 12296 | tf_op jit(solution)/shard_map/ppermute | solution.py:18
  136.5 2.5 %collective-permute-done.5 = f32[2,512]{1,0:T(2,128)S(1)} collective-permute-done((f32[2,512]{1,0:T(2,128)}, f32[2,512]{1,0:T(2,128)S(1)}, u32[]{:S(2)}, u32[]{:S(2)}) %collective-permute-start.5) | collective-permute-done | bytes 4128 | tf_op jit(solution)/shard_map/ppermute | solution.py:18
  140.9 4.5 %collective-permute-done.11 = f32[2,512]{1,0:T(2,128)S(1)} collective-permute-done((f32[2,512]{1,0:T(2,128)S(1)}, f32[2,512]{1,0:T(2,128)S(1)}, u32[]{:S(2)}, u32[]{:S(2)}) %collective-permute-start.11) | collective-permute-done | bytes 4128 | tf_op jit(solution)/shard_map/ppermute | solution.py:18
  145.4 6.6 %collective-permute-start.7 = (f32[2,512]{1,0:T(2,128)S(1)}, f32[2,512]{1,0:T(2,128)S(1)}, u32[]{:S(2)}, u32[]{:S(2)}) collective-permute-start(f32[2,512]{1,0:T(2,128)S(1)} %pad_maximum_fusion.2), channel_id=1, source_target_pairs={{1,0},{2,1},{3,2},{4,3},{5,4},{6,5},{7,6},{8,7},{9,8},{10,9},{11,1... | collective-permute-start | bytes 12296 | tf_op jit(solution)/shard_map/ppermute | solution.py:18
  155.4 2.2 %fusion.53 = f32[512,128]{1,0:T(8,128)} fusion(f32[512,512]{0,1:T(8,128)S(1)} %fusion.33, bf16[512,128]{1,0:T(8,128)(2,1)S(1)} %reshape.473, f32[512]{0:T(512)S(1)} %bitcast.197, bf16[512,256]{1,0:T(8,128)(2,1)} %collective-permute-done.6, bf16[512,256]{1,0:T(8,128)(2,1)} %collective-permute-done.4), kind=kOutput, calls=%fused_computation.79 | convolution fusion | flops 135004160 | bytes 1705984 | tf_op jit(solution)/shard_map/dot_general | solution.py:32
  165.0 2.2 %fusion.55 = f32[512,128]{1,0:T(8,128)} fusion(f32[512,512]{0,1:T(8,128)S(1)} %fusion.37, bf16[512,128]{1,0:T(8,128)(2,1)S(1)} %reshape.473, f32[512]{0:T(512)S(1)} %bitcast.196, bf16[512,256]{1,0:T(8,128)(2,1)} %collective-permute-done.10, bf16[512,256]{1,0:T(8,128)(2,1)} %collective-permute-done.8), kind=kOutput, calls=%fused_computation.81 | convolution fusion | flops 135004160 | bytes 1705984 | tf_op jit(solution)/shard_map/dot_general | solution.py:32
  174.3 2.1 %fusion.67 = f32[512,128]{1,0:T(8,128)} fusion(f32[512,128]{1,0:T(8,128)S(1)} %copy-done.15, f32[512,128]{1,0:T(8,128)S(1)} %fusion.54, f32[512,128]{1,0:T(8,128)S(1)} %copy-done.14, f32[512,128]{1,0:T(8,128)S(1)} %copy-done.12, f32[512,512]{0,1:T(8,128)S(1)} %fusion.31, bf16[512,128]{1,0:T(8,128)(2,1)S(1)} %reshape.473, f32[512]{0:T(512)S(1)} %bitcast.194, ...), kind=kOutput, calls=%fused_computation.100 | convolution fusion | flops 135331840 | bytes 2754560 | tf_op jit(solution)/shard_map/dot_general | solution.py:32
  (200 shorter events, 64.0 us)
Async XLA Ops:
  0.6 162.4 %collective-permute-start.10 = (bf16[512,256]{1,0:T(8,128)(2,1)}, bf16[512,256]{1,0:T(8,128)(2,1)}, u32[]{:S(2)}, u32[]{:S(2)}) collective-permute-start(bf16[512,256]{1,0:T(8,128)(2,1)} %param.9), channel_id=1, source_target_pairs={{2,0},{3,1},{4,2},{5,3},{6,4},{7,5},{8,6},{9,7},{10,8},{11,9},{12,... | collective-permute-start | bytes 786440 | tf_op jit(solution)/shard_map/ppermute | solution.py:18
  8.8 146.6 %collective-permute-start.6 = (bf16[512,256]{1,0:T(8,128)(2,1)}, bf16[512,256]{1,0:T(8,128)(2,1)}, u32[]{:S(2)}, u32[]{:S(2)}) collective-permute-start(bf16[512,256]{1,0:T(8,128)(2,1)} %param.9), channel_id=1, source_target_pairs={{1,0},{2,1},{3,2},{4,3},{5,4},{6,5},{7,6},{8,7},{9,8},{10,9},{11,1... | collective-permute-start | bytes 786440 | tf_op jit(solution)/shard_map/ppermute | solution.py:18
  14.8 17.8 %all-to-all-start.1 = ((bf16[32,32,128]{2,1,0:T(8,128)(2,1)}), bf16[32,32,128]{2,1,0:T(8,128)(2,1)S(1)}, u32[]{:S(2)}, u32[]{:S(2)}) async-start(bf16[32,32,128]{2,1,0:T(8,128)(2,1)} %bitcast.38), calls=%async_computation.1 | async-start | bytes 524288 | tf_op jit(solution)/shard_map/all_to_all | solution.py:140
  32.5 19.9 %all-to-all-start.2 = ((bf16[32,32,128]{2,1,0:T(8,128)(2,1)}), bf16[32,32,128]{2,1,0:T(8,128)(2,1)S(1)}, u32[]{:S(2)}, u32[]{:S(2)}) async-start(bf16[32,32,128]{2,1,0:T(8,128)(2,1)} %bitcast.42), calls=%async_computation.2 | async-start | bytes 524288 | tf_op jit(solution)/shard_map/all_to_all | solution.py:141
  44.9 59.6 %copy-start.44 = (pred[512]{0:T(512)(128)(4,1)}, pred[512]{0:T(512)(128)(4,1)S(1)}, u32[]{:S(2)}) copy-start(pred[512]{0:T(512)(128)(4,1)S(1)} %fusion.196) | copy-start | bytes 1540
  44.9 50.8 %copy-start.46 = (pred[512]{0:T(512)(128)(4,1)}, pred[512]{0:T(512)(128)(4,1)S(1)}, u32[]{:S(2)}) copy-start(pred[512]{0:T(512)(128)(4,1)S(1)} %broadcast_compare_fusion) | copy-start | bytes 1540
  45.0 65.8 %copy-start.25 = (s32[512]{0:T(512)}, s32[512]{0:T(512)S(1)}, u32[]{:S(2)}) copy-start(s32[512]{0:T(512)S(1)} %iota_add_fusion) | copy-start | bytes 6148
  52.4 22.9 %all-to-all-start = ((bf16[32,32,256]{2,1,0:T(8,128)(2,1)}), bf16[32,32,256]{2,1,0:T(8,128)(2,1)S(1)}, u32[]{:S(2)}, u32[]{:S(2)}) async-start(bf16[32,32,256]{2,1,0:T(8,128)(2,1)} %bitcast.34), calls=%async_computation | async-start | bytes 1048576 | tf_op jit(solution)/shard_map/all_to_all | solution.py:139
  58.1 26.5 %copy-start.48 = (pred[512]{0:T(512)(128)(4,1)}, pred[512]{0:T(512)(128)(4,1)S(1)}, u32[]{:S(2)}) copy-start(pred[512]{0:T(512)(128)(4,1)S(1)} %broadcast_compare_fusion.1) | copy-start | bytes 1540
  58.7 25.9 %copy-start.31 = (s32[512]{0:T(512)}, s32[512]{0:T(512)S(1)}, u32[]{:S(2)}) copy-start(s32[512]{0:T(512)S(1)} %fusion.195) | copy-start | bytes 6148
  59.5 25.2 %copy-start.41 = (s32[512]{0:T(512)}, s32[512]{0:T(512)S(1)}, u32[]{:S(2)}) copy-start(s32[512]{0:T(512)S(1)} %get-tuple-element.17) | copy-start | bytes 6148
  59.5 36.3 %copy-start.39 = (s32[512]{0:T(512)}, s32[512]{0:T(512)S(1)}, u32[]{:S(2)}) copy-start(s32[512]{0:T(512)S(1)} %get-tuple-element.18) | copy-start | bytes 6148
  59.5 45.1 %copy-start.35 = (s32[512]{0:T(512)}, s32[512]{0:T(512)S(1)}, u32[]{:S(2)}) copy-start(s32[512]{0:T(512)S(1)} %get-tuple-element.20) | copy-start | bytes 6148
  59.8 46.2 %collective-permute-start.3 = (bf16[512,128]{1,0:T(8,128)(2,1)S(1)}, bf16[512,128]{1,0:T(8,128)(2,1)S(1)}, u32[]{:S(2)}, u32[]{:S(2)}) collective-permute-start(bf16[512,128]{1,0:T(8,128)(2,1)S(1)} %reshape.473), channel_id=1, source_target_pairs={{0,2},{1,3},{2,4},{3,5},{4,6},{5,7},{6,8},{7,9},{8,10},{9,11},{10,... | collective-permute-start | bytes 393224 | tf_op jit(solution)/shard_map/ppermute | solution.py:18
  64.1 34.1 %collective-permute-start.2 = (bf16[512,128]{1,0:T(8,128)(2,1)S(1)}, bf16[512,128]{1,0:T(8,128)(2,1)S(1)}, u32[]{:S(2)}, u32[]{:S(2)}) collective-permute-start(bf16[512,128]{1,0:T(8,128)(2,1)S(1)} %reshape.473), channel_id=1, source_target_pairs={{0,1},{1,2},{2,3},{3,4},{4,5},{5,6},{6,7},{7,8},{8,9},{9,10},{10,1... | collective-permute-start | bytes 393224 | tf_op jit(solution)/shard_map/ppermute | solution.py:18
  67.8 40.4 %copy-start.8 = (bf16[512,128]{1,0:T(8,128)(2,1)}, bf16[512,128]{1,0:T(8,128)(2,1)S(1)}, u32[]{:S(2)}) copy-start(bf16[512,128]{1,0:T(8,128)(2,1)S(1)} %reshape.470) | copy-start | bytes 393220
  67.8 14.7 %collective-permute-start = (bf16[512,128]{1,0:T(8,128)(2,1)S(1)}, bf16[512,128]{1,0:T(8,128)(2,1)S(1)}, u32[]{:S(2)}, u32[]{:S(2)}) collective-permute-start(bf16[512,128]{1,0:T(8,128)(2,1)S(1)} %reshape.470), channel_id=1, source_target_pairs={{0,1},{1,2},{2,3},{3,4},{4,5},{5,6},{6,7},{7,8},{8,9},{9,10},{10,1... | collective-permute-start | bytes 393224 | tf_op jit(solution)/shard_map/ppermute | solution.py:18
  82.5 10.6 %collective-permute-start.1 = (bf16[512,128]{1,0:T(8,128)(2,1)S(1)}, bf16[512,128]{1,0:T(8,128)(2,1)S(1)}, u32[]{:S(2)}, u32[]{:S(2)}) collective-permute-start(bf16[512,128]{1,0:T(8,128)(2,1)S(1)} %reshape.470), channel_id=1, source_target_pairs={{0,2},{1,3},{2,4},{3,5},{4,6},{5,7},{6,8},{7,9},{8,10},{9,11},{10,... | collective-permute-start | bytes 393224 | tf_op jit(solution)/shard_map/ppermute | solution.py:18
  93.1 66.0 %collective-permute-start.8 = (bf16[512,256]{1,0:T(8,128)(2,1)}, bf16[512,256]{1,0:T(8,128)(2,1)}, u32[]{:S(2)}, u32[]{:S(2)}) collective-permute-start(bf16[512,256]{1,0:T(8,128)(2,1)} %reshape.467), channel_id=1, source_target_pairs={{2,0},{3,1},{4,2},{5,3},{6,4},{7,5},{8,6},{9,7},{10,8},{11,9},{12,... | collective-permute-start | bytes 786440 | tf_op jit(solution)/shard_map/ppermute | solution.py:18
  98.2 55.1 %collective-permute-start.4 = (bf16[512,256]{1,0:T(8,128)(2,1)}, bf16[512,256]{1,0:T(8,128)(2,1)}, u32[]{:S(2)}, u32[]{:S(2)}) collective-permute-start(bf16[512,256]{1,0:T(8,128)(2,1)} %reshape.467), channel_id=1, source_target_pairs={{1,0},{2,1},{3,2},{4,3},{5,4},{6,5},{7,6},{8,7},{9,8},{10,9},{11,1... | collective-permute-start | bytes 786440 | tf_op jit(solution)/shard_map/ppermute | solution.py:18
  117.8 15.5 %collective-permute-start.9 = (f32[2,512]{1,0:T(2,128)}, f32[2,512]{1,0:T(2,128)}, u32[]{:S(2)}, u32[]{:S(2)}) collective-permute-start(f32[2,512]{1,0:T(2,128)} %pad_maximum_fusion.1), channel_id=1, source_target_pairs={{2,0},{3,1},{4,2},{5,3},{6,4},{7,5},{8,6},{9,7},{10,8},{11,9},{12,... | collective-permute-start | bytes 12296 | tf_op jit(solution)/shard_map/ppermute | solution.py:18
  133.3 5.7 %collective-permute-start.5 = (f32[2,512]{1,0:T(2,128)}, f32[2,512]{1,0:T(2,128)S(1)}, u32[]{:S(2)}, u32[]{:S(2)}) collective-permute-start(f32[2,512]{1,0:T(2,128)} %pad_maximum_fusion.1), channel_id=1, source_target_pairs={{1,0},{2,1},{3,2},{4,3},{5,4},{6,5},{7,6},{8,7},{9,8},{10,9},{11,1... | collective-permute-start | bytes 12296 | tf_op jit(solution)/shard_map/ppermute | solution.py:18
  139.0 6.4 %collective-permute-start.11 = (f32[2,512]{1,0:T(2,128)S(1)}, f32[2,512]{1,0:T(2,128)S(1)}, u32[]{:S(2)}, u32[]{:S(2)}) collective-permute-start(f32[2,512]{1,0:T(2,128)S(1)} %pad_maximum_fusion.2), channel_id=1, source_target_pairs={{2,0},{3,1},{4,2},{5,3},{6,4},{7,5},{8,6},{9,7},{10,8},{11,9},{12,... | collective-permute-start | bytes 12296 | tf_op jit(solution)/shard_map/ppermute | solution.py:18
  145.4 7.9 %collective-permute-start.7 = (f32[2,512]{1,0:T(2,128)S(1)}, f32[2,512]{1,0:T(2,128)S(1)}, u32[]{:S(2)}, u32[]{:S(2)}) collective-permute-start(f32[2,512]{1,0:T(2,128)S(1)} %pad_maximum_fusion.2), channel_id=1, source_target_pairs={{1,0},{2,1},{3,2},{4,3},{5,4},{6,5},{7,6},{8,7},{9,8},{10,9},{11,1... | collective-permute-start | bytes 12296 | tf_op jit(solution)/shard_map/ppermute | solution.py:18
  (41 other events, 169.0 us)
where the time goes:
time: 178 us; the launch traced here: 176 us
  starting transfers between devices  69 us (39%)
  matrix products  46.9 us (26%)
  waiting for transfers between devices  38.4 us (22%)
  local copies, waits for them, and re-layouts  16.2 us (9%)
  other arithmetic  4.33 us (2%)
    ppermute x12, starting transfers between devices, from_behind(): lax.ppermute(value, axis, [(source, source + steps) for source in range(f...  47.1 us
    dot_general x12, matrix products, contract_rows(): lax.dot_general(left, right, (((0,), (0,)), ((), ())), preferred_element_...  20.3 us
    ppermute x12, waiting for transfers between devices, from_behind(): lax.ppermute(value, axis, [(source, source + steps) for source in range(f...  19.5 us
    dot_general x10, matrix products, head_scores(): lax.dot_general(query_head, key_block, (((1,), (1,)), ((), ())), preferre...  13.8 us
    unnamed x109, local copies, waits for them, and re-layouts  13.2 us
    all_to_all x1, starting transfers between devices, on_device(): lax.all_to_all(value_out, 'ctx', split_axis=0, concat_axis=0, tiled=True)  9.42 us
    all_to_all x1, waiting for transfers between devices, on_device(): lax.all_to_all(key_out, 'ctx', split_axis=0, concat_axis=0, tiled=True)  8.41 us
    all_to_all x1, waiting for transfers between devices, on_device(): lax.all_to_all(value_out, 'ctx', split_axis=0, concat_axis=0, tiled=True)  7.45 us
  transfers between devices with their start and end apart: 15, of which 8 were waited for; matrix products, arithmetic and copies ran while one was open for 26% of the time, Pallas kernels for 0%

commit v1 on v0

v1 whole, which is shorter than its diff:
```python
import functools

import jax
import jax.numpy as jnp
from jax import lax
from jax.experimental import pallas as pl
from jax.experimental.pallas import tpu as pltpu
from jax.sharding import PartitionSpec as P

N = 32
NZ = 8
NX = 4
BLK = 32
PER = 16
ROWS = 512
HD = 128
WIN = 3 * ROWS
TILE = 256
NEGATIVE = -1e30
LOG2E = 1.4426950408889634
FACTOR = HD**-0.5
MESH = pl.DeviceIdType.MESH
BF = jnp.bfloat16
F32 = jnp.float32


def peer(index):
    return (lax.axis_index("dp"), index)


def near_first(count, step):
    return jnp.where(step % 2 == 1, (step + 1) // 2, (count - step // 2) % count)


def target_of(me, step):
    z = (me % NZ + near_first(NZ, step // NX)) % NZ
    x = (me // NZ + near_first(NX, step % NX)) % NX
    return x * NZ + z


def send(src, dst, send_sem, recv_sem, index):
    return pltpu.make_async_remote_copy(
        src, dst, send_sem, recv_sem, device_id=peer(index), device_id_type=MESH
    )


def gather_kernel(
    send_ids, recv_ids, q_ref, k_ref, v_ref, q_out, kv_out,
    kv_send, kv_recv, q_send, q_recv, window,
    kv_ssem, kv_rsem, q_ssem, q_rsem, h1_ssem, h1_rsem, h2_ssem, h2_rsem,
):
    me = lax.axis_index("ctx")
    right = (me + 1) % N
    barrier = pltpu.get_barrier_semaphore()

    def greet(step, carry):
        pl.semaphore_signal(
            barrier, inc=1, device_id=peer((me + step) % N), device_id_type=MESH
        )
        return carry

    lax.fori_loop(1, N, greet, 0)

    def pack(dest, carry):
        held = send_ids[dest]
        kv_send[dest, :, :HD] = k_ref[held]
        kv_send[dest, :, HD:] = v_ref[held]
        q_send[dest] = q_ref[held]
        return carry

    lax.fori_loop(0, N, pack, 0)
    kv_recv[me] = kv_send[me]
    q_recv[me] = q_send[me]
    pl.semaphore_wait(barrier, N - 1)

    def push_kv(step, carry):
        dest = target_of(me, step)
        send(kv_send.at[dest], kv_recv.at[me], kv_ssem, kv_rsem, dest).start()
        return carry

    def push_q(step, carry):
        dest = target_of(me, step)
        send(q_send.at[dest], q_recv.at[me], q_ssem, q_rsem, dest).start()
        return carry

    lax.fori_loop(1, N, push_kv, 0)
    lax.fori_loop(1, N, push_q, 0)

    def drain(buf, sem):
        part = buf.at[pl.ds(0, N - 1)]
        pltpu.make_async_copy(part, part, sem).wait()

    drain(kv_recv, kv_rsem)

    def unpack_kv(block, carry):
        window[pl.ds(pl.multiple_of(2 * ROWS + block * BLK, BLK), BLK)] = kv_recv[recv_ids[block]]
        return carry

    lax.fori_loop(0, PER, unpack_kv, 0)
    chunks = 4
    size = ROWS // chunks

    def hop(level, chunk, ssem, rsem):
        return send(
            window.at[pl.ds((2 - level) * ROWS + chunk * size, size)],
            window.at[pl.ds((1 - level) * ROWS + chunk * size, size)],
            ssem.at[chunk], rsem.at[chunk], right,
        )

    first = [hop(0, chunk, h1_ssem, h1_rsem) for chunk in range(chunks)]
    second = [hop(1, chunk, h2_ssem, h2_rsem) for chunk in range(chunks)]
    for copy in first:
        copy.start()
    for copy, onward in zip(first, second):
        copy.wait_recv()
        onward.start()
    drain(q_recv, q_rsem)

    def unpack_q(block, carry):
        q_out[pl.ds(pl.multiple_of(block * BLK, BLK), BLK)] = q_recv[recv_ids[block]]
        return carry

    lax.fori_loop(0, PER, unpack_q, 0)
    for copy in second:
        copy.wait_recv()
    kv_out[...] = window[...]
    for copy in first + second:
        copy.wait_send()
    drain(kv_send, kv_ssem)
    drain(q_send, q_ssem)


def compute_kernel(
    start_ref, q_ref, kv_ref, g_ref, att_ref, dq_ref, own_ref, mid_ref, far_ref,
    kt, vt, dkv,
):
    kt[...] = kv_ref[:, :HD].T
    vt[...] = kv_ref[:, HD:].T
    dkv[...] = jnp.zeros_like(dkv)
    span = 5 * TILE

    def step(index, carry):
        head, row = index // 2, index % 2
        rows = pl.ds(pl.multiple_of(row * TILE, TILE), TILE)
        cols = pl.ds(pl.multiple_of(head * HD, HD), HD)
        keys = pl.ds(pl.multiple_of(row * TILE, TILE), span)
        q = q_ref[rows, cols]
        g = g_ref[rows, cols]
        k = kv_ref[keys, :HD]
        v = kv_ref[keys, HD:]
        raw = lax.dot_general(k, q, (((1,), (1,)), ((), ())), preferred_element_type=F32)
        start = start_ref[:, rows] - row * TILE
        pos = lax.broadcasted_iota(jnp.int32, (span, TILE), 0)
        query = lax.broadcasted_iota(jnp.int32, (span, TILE), 1) + 4 * TILE
        scores = jnp.where((pos >= start) & (pos <= query), raw * (FACTOR * LOG2E), NEGATIVE)
        peak = jnp.max(scores, axis=0, keepdims=True)
        weights = jnp.exp2(scores - peak)
        total = jnp.sum(weights, axis=0, keepdims=True)
        weights = weights * (1.0 / total)
        low = weights.astype(BF)
        out = jnp.dot(vt[:, keys], low, preferred_element_type=F32).astype(BF)
        att_ref[rows, cols] = out.T
        gt = g.T.astype(F32)
        delta = jnp.sum(gt * out.astype(F32), axis=0, keepdims=True)
        dprobs = lax.dot_general(v, g, (((1,), (1,)), ((), ())), preferred_element_type=F32)
        dscores = (weights * (dprobs - delta)).astype(BF)
        dkv[keys, :HD] += jnp.dot(dscores, q, preferred_element_type=F32)
        dkv[keys, HD:] += jnp.dot(low, g, preferred_element_type=F32)
        dq = jnp.dot(kt[:, keys], dscores, preferred_element_type=F32) * FACTOR
        dq_ref[rows, cols] = dq.T
        return carry

    lax.fori_loop(0, 4, step, 0)
    dkv[:, :HD] = dkv[:, :HD] * FACTOR
    far_ref[...] = dkv[:ROWS].astype(BF)
    mid_ref[...] = dkv[ROWS : 2 * ROWS].astype(BF)
    own_ref[...] = dkv[2 * ROWS :]


def return_kernel(
    own_ref, mid_ref, far_ref, dk_ref, dv_ref, got_far, total, got_mid,
    s2_sem, r2_sem, s1_sem, r1_sem,
):
    me = lax.axis_index("ctx")
    left = (me + N - 1) % N
    right = (me + 1) % N
    barrier = pltpu.get_barrier_semaphore()
    for other in (left, right):
        pl.semaphore_signal(barrier, inc=1, device_id=peer(other), device_id_type=MESH)
    pl.semaphore_wait(barrier, 2)
    chunks = 4
    size = ROWS // chunks
    first = []
    second = []
    for chunk in range(chunks):
        part = pl.ds(chunk * size, size)
        first.append(send(far_ref.at[part], got_far.at[part], s2_sem.at[chunk], r2_sem.at[chunk], left))
        second.append(send(total.at[part], got_mid.at[part], s1_sem.at[chunk], r1_sem.at[chunk], left))
    for copy in first:
        copy.start()
    for chunk in range(chunks):
        part = pl.ds(chunk * size, size)
        first[chunk].wait_recv()
        total[part] = (mid_ref[part].astype(F32) + got_far[part].astype(F32)).astype(BF)
        second[chunk].start()
    for chunk in range(chunks):
        part = pl.ds(chunk * size, size)
        second[chunk].wait_recv()
        whole = own_ref[part] + got_mid[part].astype(F32)
        dk_ref[part] = whole[:, :HD]
        dv_ref[part] = whole[:, HD:]
    for copy in first + second:
        copy.wait_send()


def vmem(count):
    return [pl.BlockSpec(memory_space=pltpu.VMEM)] * count


def shape(*dims, dtype=BF):
    return jax.ShapeDtypeStruct(dims, dtype)


def on_device(queries, keys, values, cotangent, doc_lengths, old_slots):
    me = lax.axis_index("ctx")
    table = old_slots.reshape(N, PER)
    send_ids = jnp.sum(jnp.where(table // PER == me, table % PER, 0), axis=1)
    recv_ids = lax.dynamic_slice_in_dim(old_slots, me * PER, PER) // PER
    ends = jnp.cumsum(doc_lengths)
    starts = ends - doc_lengths
    pos = me * ROWS + jnp.arange(ROWS, dtype=jnp.int32)
    start = jnp.max(jnp.where(starts[:, None] <= pos[None, :], starts[:, None], 0), axis=0)
    start = (start - me * ROWS + 2 * ROWS).reshape(1, ROWS)

    smem = [pl.BlockSpec(memory_space=pltpu.SMEM)] * 2
    dma = pltpu.SemaphoreType.DMA
    buf = lambda *dims: pltpu.VMEM(dims, BF)
    q_new, kv = pl.pallas_call(
        gather_kernel,
        out_shape=[shape(ROWS, 2 * HD), shape(WIN, 2 * HD)],
        in_specs=smem + vmem(3),
        out_specs=vmem(2),
        scratch_shapes=[buf(N, BLK, 2 * HD)] * 4 + [buf(WIN, 2 * HD)]
        + [dma(())] * 4 + [dma((4,))] * 4,
        compiler_params=pltpu.CompilerParams(
            collective_id=0, has_side_effects=True, vmem_limit_bytes=32 << 20
        ),
        name="gather",
    )(
        send_ids, recv_ids,
        queries.reshape(PER, BLK, 2 * HD),
        keys.reshape(PER, BLK, HD),
        values.reshape(PER, BLK, HD),
    )
    attended, query_grad, own, mid, far = pl.pallas_call(
        compute_kernel,
        out_shape=[
            shape(ROWS, 2 * HD),
            shape(ROWS, 2 * HD, dtype=F32),
            shape(ROWS, 2 * HD, dtype=F32),
            shape(ROWS, 2 * HD),
            shape(ROWS, 2 * HD),
        ],
        in_specs=vmem(4),
        out_specs=vmem(5),
        scratch_shapes=[buf(HD, WIN), buf(HD, WIN), pltpu.VMEM((WIN, 2 * HD), F32)],
        compiler_params=pltpu.CompilerParams(vmem_limit_bytes=48 << 20),
        name="attend",
    )(start, q_new, kv, cotangent)
    key_grad, value_grad = pl.pallas_call(
        return_kernel,
        out_shape=[shape(ROWS, HD, dtype=F32)] * 2,
        in_specs=vmem(3),
        out_specs=vmem(2),
        scratch_shapes=[buf(ROWS, 2 * HD)] * 3 + [dma((4,))] * 4,
        compiler_params=pltpu.CompilerParams(
            collective_id=1, has_side_effects=True, vmem_limit_bytes=32 << 20
        ),
        name="give_back",
    )(own, mid, far)
    return attended, query_grad, key_grad, value_grad


def solution(mesh):
    rows = P(("dp", "ctx"), None)
    return jax.shard_map(
        on_device,
        mesh=mesh,
        in_specs=(rows, rows, rows, rows, P("dp"), P("dp")),
        out_specs=(rows, rows, rows, rows),
        check_vma=False,
    )
```

time: 178 us -> 75.5 us (0.42)
  starting transfers between devices: 69 us -> 0 us
  Pallas kernels: 0 us -> 67.5 us
  matrix products: 46.9 us -> 0 us
  waiting for transfers between devices: 38.4 us -> 0 us
  local copies, waits for them, and re-layouts: 16.2 us -> 5.32 us
  other arithmetic: 4.33 us -> 1.24 us
    pallas_call x0 -> x3, Pallas kernels: none -> 67.5 us  [the longest x1 45.4 us: on_device(): pl.pallas_call(gather_kernel, out_shape=[shape(ROWS, 2 * HD), shape(WIN,...]
    ppermute x12 -> x0, starting transfers between devices: 47.1 us -> none  [from_behind(): lax.ppermute(value, axis, [(source, source + steps) for source in range(f...]
    dot_general x42 -> x0, matrix products: 46.9 us -> none  [the longest x12 20.3 us: contract_rows(): lax.dot_general(left, right, (((0,), (0,)), ((), ())), preferred_element_...]
    all_to_all x3 -> x0, starting transfers between devices: 21.8 us -> none  [the longest x1 9.42 us: on_device(): lax.all_to_all(value_out, 'ctx', split_axis=0, concat_axis=0, tiled=True)]
    ppermute x12 -> x0, waiting for transfers between devices: 19.5 us -> none  [from_behind(): lax.ppermute(value, axis, [(source, source + steps) for source in range(f...]
    all_to_all x3 -> x0, waiting for transfers between devices: 18.8 us -> none  [the longest x1 8.41 us: on_device(): lax.all_to_all(key_out, 'ctx', split_axis=0, concat_axis=0, tiled=True)]
    unnamed x109 -> x12, local copies, waits for them, and re-layouts: 13.2 us -> 3.81 us
    reduce_sum x10 -> x1, other arithmetic: 2.48 us -> 0.13 us  [on_device(): send_ids = jnp.sum(jnp.where(table // PER == me, table % PER, 0), axis=1)]
  transfers between devices with their start and end apart: 15 -> 0, of which waited for: 8 -> 0; matrix products, arithmetic and copies ran while one was open for 26% -> 0% of each run, Pallas kernels for 0% -> 0%
where the time goes in v1:
time: 75.5 us; the launch traced here: 74.7 us
  Pallas kernels  67.5 us (89%)
  local copies, waits for them, and re-layouts  5.32 us (7%)
  other arithmetic  1.24 us (2%)
    pallas_call x1, Pallas kernels, on_device(): pl.pallas_call(gather_kernel, out_shape=[shape(ROWS, 2 * HD), shape(WIN,...  45.4 us
    pallas_call x1, Pallas kernels, on_device(): pl.pallas_call(return_kernel, out_shape=[shape(ROWS, HD, dtype=F32)] * 2,...  13.3 us
    pallas_call x1, Pallas kernels, on_device(): pl.pallas_call(compute_kernel, out_shape=[shape(ROWS, 2 * HD), shape(ROWS...  8.73 us
    unnamed x12, local copies, waits for them, and re-layouts  3.81 us

profile of v1, /device:TPU:10, one launch (start us, length us, event | category | flops | bytes accessed | tf_op | source)
XLA Modules:
  0.0 74.7 jit_solution(9073487371829236757)
XLA Ops:
  0.6 0.0 copy-start.2
  0.6 0.8 %and_select_fusion.recv_ids = s32[16]{0:T(128)S(1)} fusion(s32[512]{0:T(512)} %param.11, s32[]{:T(128)S(6)} %select_n.32), kind=kLoop, calls=%fused_computation.14 | loop fusion | flops 240 | bytes 132 | tf_op jit(solution)/shard_map/jit(floor_divide)/jit(_where)/select_n | solution.py:228
  1.4 0.8 %reshape.68 = s32[32,16]{1,0:T(8,128)S(1)} reshape(s32[512]{0:T(512)} %param.11) | data formatting | bytes 4096 | tf_op jit(solution)/shard_map/reshape | solution.py:226
  2.2 0.1 fusion.2.send_ids
  2.3 0.8 %copy.12 = s32[64,1]{1,0:T(8,128)S(1)} copy(s32[64,1]{0,1:T(1,128)} %bitcast.9) | data formatting | bytes 512 | tf_op jit(solution)/shard_map/reshape.42
  3.1 0.1 reduce-window.9
  3.2 0.0 copy-start.4
  3.2 0.1 reduce
  3.3 0.5 copy-done.4
  3.8 0.1 select_reduce_fusion
  4.0 0.0 copy-done.2
  4.0 0.0 copy-start.1
  4.0 0.9 %copy-done.1 = bf16[512,256]{1,0:T(8,128)(2,1)S(1)} copy-done((bf16[512,256]{1,0:T(8,128)(2,1)S(1)}, bf16[512,256]{1,0:T(8,128)(2,1)}, u32[]{:S(2)}) %copy-start.1) | copy-done | bytes 262168
  4.9 0.0 copy-start.3
  4.9 0.9 %copy-done.3 = bf16[512,128]{1,0:T(8,128)(2,1)S(1)} copy-done((bf16[512,128]{1,0:T(8,128)(2,1)S(1)}, bf16[512,128]{1,0:T(8,128)(2,1)}, u32[]{:S(2)}) %copy-start.3) | copy-done | bytes 131096
  5.8 0.0 copy-start
  5.8 45.4 %gather.1 = (bf16[512,256]{1,0:T(8,128)(2,1)S(1)}, bf16[1536,256]{1,0:T(8,128)(2,1)S(1)}) custom-call(s32[32]{0:T(128)S(1)} %fusion.2.send_ids, s32[16]{0:T(128)S(1)} %and_select_fusion.recv_ids, bf16[16,32,256]{2,1,0:T(8,128)(2,1)S(1)} %bitcast.5, bf16[16,32,128]{2,1,0:T(8,128)(2,1)S(1)} %bitcast.6, bf16[16,32,128]{2,1,0:T(8,128)(2,1)S(1)} %bitcast.7), custom_call_target="tpu_custom_call" | custom-call | tf_op jit(solution)/shard_map/gather/pallas_call | solution.py:238
  51.3 0.0 copy-done
  51.3 8.7 %attend.1 = (bf16[512,256]{1,0:T(8,128)(2,1)}, f32[512,256]{1,0:T(8,128)}, f32[512,256]{1,0:T(8,128)S(1)}, bf16[512,256]{1,0:T(8,128)(2,1)S(1)}, bf16[512,256]{1,0:T(8,128)(2,1)S(1)}) custom-call(s32[1,512]{1,0:T(1,128)S(1)} %bitcast.8, bf16[512,256]{1,0:T(8,128)(2,1)S(1)} %get-tuple-element.13.q_ref, bf16[1536,256]{1,0:T(8,128)(2,1)S(1)} %get-tuple-element.14.kv_ref, ...), custom_call_target="tpu_custom_call" | custom-call | tf_op jit(solution)/shard_map/attend/pallas_call | solution.py:255
  60.0 13.3 %give_back.1 = (f32[512,128]{1,0:T(8,128)S(1)}, f32[512,128]{1,0:T(8,128)S(1)}) custom-call(f32[512,256]{1,0:T(8,128)S(1)} %get-tuple-element.17.own_ref, bf16[512,256]{1,0:T(8,128)(2,1)S(1)} %get-tuple-element.18.mid_ref, bf16[512,256]{1,0:T(8,128)(2,1)S(1)} %get-tuple-element.19.far_ref), custom_call_target="tpu_custom_call" | custom-call | tf_op jit(solution)/shard_map/give_back/pallas_call | solution.py:270
  73.3 0.7 copy.15
  74.0 0.7 copy.16
  (3 shorter events, 0.0 us)
Async XLA Ops:
  0.6 3.3 %copy-start.2 = (bf16[512,128]{1,0:T(8,128)(2,1)S(1)}, bf16[512,128]{1,0:T(8,128)(2,1)}, u32[]{:S(2)}) copy-start(bf16[512,128]{1,0:T(8,128)(2,1)} %param.7) | copy-start | bytes 393220
  3.2 0.7 copy-start.4
  4.0 1.0 %copy-start.1 = (bf16[512,256]{1,0:T(8,128)(2,1)S(1)}, bf16[512,256]{1,0:T(8,128)(2,1)}, u32[]{:S(2)}) copy-start(bf16[512,256]{1,0:T(8,128)(2,1)} %param.6) | copy-start | bytes 786436
  4.9 0.9 %copy-start.3 = (bf16[512,128]{1,0:T(8,128)(2,1)S(1)}, bf16[512,128]{1,0:T(8,128)(2,1)}, u32[]{:S(2)}) copy-start(bf16[512,128]{1,0:T(8,128)(2,1)} %param.8) | copy-start | bytes 393220
  5.8 45.5 %copy-start = (bf16[512,256]{1,0:T(8,128)(2,1)S(1)}, bf16[512,256]{1,0:T(8,128)(2,1)}, u32[]{:S(2)}) copy-start(bf16[512,256]{1,0:T(8,128)(2,1)} %g_ref.1) | copy-start | bytes 786436

commit v2 on v1

v2 whole, which is shorter than its diff:
```python
import jax
import jax.numpy as jnp
from jax import lax
from jax.experimental import pallas as pl
from jax.experimental.pallas import tpu as pltpu
from jax.sharding import PartitionSpec as P

N = 32
NZ = 8
NX = 4
BLK = 32
PER = 16
ROWS = 512
HD = 128
HEADS = 2
WIN = 3 * ROWS
TILE = 256
COLS = HEADS * ROWS
NDOCS = 64
CHUNKS = 4
SIZE = ROWS // CHUNKS
NEGATIVE = -1e30
LOG2E = 1.4426950408889634
FACTOR = HD**-0.5
MESH = pl.DeviceIdType.MESH
BF = jnp.bfloat16
F32 = jnp.float32
BEHIND = (7, 6, 5)
AHEAD = (1, 2, 3)


def peer(index):
    return (lax.axis_index("dp"), index)


def send(src, dst, send_sem, recv_sem, index):
    return pltpu.make_async_remote_copy(
        src, dst, send_sem, recv_sem, device_id=peer(index), device_id_type=MESH
    )


def near_first(step):
    return jnp.where(step < 2, step, 5 - step)


def dot_nt(left, right):
    return lax.dot_general(left, right, (((1,), (1,)), ((), ())), preferred_element_type=F32)


def dot(left, right):
    return jnp.dot(left, right, preferred_element_type=F32)


class Exchange:
    def __init__(self, me, out, into, mid, out_sem, in_sem, mid_sem, onward_sem):
        self.me = me
        self.out, self.into, self.mid = out, into, mid
        self.out_sem, self.in_sem = out_sem, in_sem
        self.mid_sem, self.onward_sem = mid_sem, onward_sem

    def at(self, dx, dz):
        x = (self.me // NZ + dx) % NX
        z = (self.me % NZ + dz) % NZ
        return x * NZ + z

    def push(self, dz):
        def body(step, carry):
            dest = self.at(near_first(step), dz)
            send(self.out.at[dest], self.into.at[self.me], self.out_sem, self.in_sem, dest).start()
            return carry

        lax.fori_loop(1 if dz == 0 else 0, NX, body, 0)

    def push_far(self):
        def body(step, carry):
            dx = near_first(step)
            dest = self.at(dx, NZ // 2)
            way = self.at(dx, NZ - 2)
            send(self.out.at[dest], self.mid.at[step], self.out_sem, self.mid_sem, way).start()
            return carry

        lax.fori_loop(0, NX, body, 0)

    def pass_on(self):
        pltpu.make_async_copy(self.mid, self.mid, self.mid_sem).wait()
        dest = self.at(0, NZ - 2)

        def body(step, carry):
            source = self.at(NX - near_first(step), 2)
            send(self.mid.at[step], self.into.at[source], self.onward_sem, self.in_sem, dest).start()
            return carry

        lax.fori_loop(0, NX, body, 0)

    def received(self):
        part = self.into.at[pl.ds(0, N - 1)]
        pltpu.make_async_copy(part, part, self.in_sem).wait()

    def sent(self):
        part = self.out.at[pl.ds(0, N - 1)]
        pltpu.make_async_copy(part, part, self.out_sem).wait()
        pltpu.make_async_copy(self.mid, self.mid, self.onward_sem).wait()


def main_kernel(
    slots, lengths, q_hbm, k_hbm, v_hbm, g_hbm,
    att_ref, dq_ref, own_ref, got_mid,
    q_old, k_old, v_old, g_old, held_ids,
    kv_out, kv_into, kv_mid, q_out, q_into, q_mid,
    window, kt, vt, qs, gs, gt, starts,
    probs, dprobs, low, dscores, near_out, stats,
    far_out, got_far, mid_out,
    load_sem, kv_out_sem, kv_in_sem, kv_mid_sem, kv_on_sem, q_out_sem, q_in_sem, q_mid_sem, q_on_sem,
    h1_out, h1_in, h2_out, h2_in, f_out, f_in, m_out, m_in,
):
    me = lax.axis_index("ctx")
    left = (me + N - 1) % N
    right = (me + 1) % N
    loads = [
        pltpu.make_async_copy(src, dst, load_sem.at[i])
        for i, (src, dst) in enumerate(
            ((k_hbm, k_old), (v_hbm, v_old), (q_hbm, q_old), (g_hbm, g_old))
        )
    ]
    for load in loads:
        load.start()
    barrier = pltpu.get_barrier_semaphore()

    def greet(step, carry):
        pl.semaphore_signal(barrier, inc=1, device_id=peer((me + step) % N), device_id_type=MESH)
        return carry

    lax.fori_loop(1, N, greet, 0)

    def find(dest, carry):
        held = 0
        for j in range(PER):
            slot = slots[dest * PER + j]
            held = held + jnp.where(slot // PER == me, slot % PER, 0)
        held_ids[dest] = held
        return carry

    lax.fori_loop(0, N, find, 0)
    loads[0].wait()
    loads[1].wait()

    def pack_kv(dest, carry):
        held = held_ids[dest]
        kv_out[dest, :, :HD] = k_old[held]
        kv_out[dest, :, HD:] = v_old[held]
        return carry

    lax.fori_loop(0, N, pack_kv, 0)
    loads[2].wait()

    def pack_q(dest, carry):
        q_out[dest] = q_old[held_ids[dest]]
        return carry

    lax.fori_loop(0, N, pack_q, 0)
    kv_into[me] = kv_out[me]
    q_into[me] = q_out[me]
    pl.semaphore_wait(barrier, N - 1)

    kvs = Exchange(me, kv_out, kv_into, kv_mid, kv_out_sem, kv_in_sem, kv_mid_sem, kv_on_sem)
    queries = Exchange(me, q_out, q_into, q_mid, q_out_sem, q_in_sem, q_mid_sem, q_on_sem)
    kvs.push_far()
    kvs.push(0)
    for ahead, behind in zip(AHEAD, BEHIND):
        kvs.push(ahead)
        kvs.push(behind)
    kvs.pass_on()
    queries.push_far()
    queries.push(0)
    for behind in BEHIND:
        queries.push(behind)
    queries.pass_on()

    loads[3].wait()
    for half in range(2):
        for head in range(HEADS):
            cols = slice(half * ROWS + head * TILE, half * ROWS + (head + 1) * TILE)
            part = g_old[half * TILE : (half + 1) * TILE, head * HD : (head + 1) * HD]
            gs[cols] = part
            gt[:, cols] = part.T
    pos = lax.broadcasted_iota(jnp.int32, (1, ROWS), 1) + me * ROWS

    def find_start(doc, carry):
        begin, found = carry
        found = jnp.where(begin <= pos, begin, found)
        return begin + lengths[doc], found

    _, found = lax.fori_loop(0, NDOCS, find_start, (jnp.int32(0), jnp.zeros((1, ROWS), jnp.int32)))
    starts[...] = found - me * ROWS + 2 * ROWS

    kvs.received()

    def unpack_kv(block, carry):
        source = slots[me * PER + block] // PER
        window[pl.ds(pl.multiple_of(2 * ROWS + block * BLK, BLK), BLK)] = kv_into[source]
        return carry

    lax.fori_loop(0, PER, unpack_kv, 0)

    def hop(level, chunk, out_sem, in_sem):
        return send(
            window.at[pl.ds((2 - level) * ROWS + chunk * SIZE, SIZE)],
            window.at[pl.ds((1 - level) * ROWS + chunk * SIZE, SIZE)],
            out_sem.at[chunk], in_sem.at[chunk], right,
        )

    first = [hop(0, chunk, h1_out, h1_in) for chunk in range(CHUNKS)]
    second = [hop(1, chunk, h2_out, h2_in) for chunk in range(CHUNKS)]
    for copy in first:
        copy.start()
    for ahead in AHEAD:
        queries.push(ahead)
    for copy, onward in zip(first, second):
        copy.wait_recv()
        onward.start()
    kt[:, ROWS:] = window[ROWS:, :HD].T
    vt[:, ROWS:] = window[ROWS:, HD:].T

    def columns(half, head):
        return pl.ds(pl.multiple_of(half * ROWS + head * TILE, TILE), TILE)

    def near_rows(half):
        return slice(ROWS, 2 * ROWS + (half + 1) * TILE)

    def near_dprobs(half):
        rows = near_rows(half)

        def body(head, carry):
            cols = columns(half, head)
            dprobs[rows, cols] = dot_nt(window[rows, HD:], gs[cols])
            return carry

        lax.fori_loop(0, HEADS, body, 0)

    near_dprobs(0)
    near_dprobs(1)
    queries.received()

    def unpack_q(block, carry):
        source = slots[me * PER + block] // PER
        row = (block // 8) * ROWS + (block % 8) * BLK
        qs[pl.ds(pl.multiple_of(row, BLK), BLK)] = q_into[source, :, :HD]
        qs[pl.ds(pl.multiple_of(row + TILE, BLK), BLK)] = q_into[source, :, HD:]
        return carry

    lax.fori_loop(0, PER, unpack_q, 0)

    def near_forward(half):
        rows = near_rows(half)
        size = rows.stop - rows.start
        pos = lax.broadcasted_iota(jnp.int32, (size, TILE), 0) + ROWS
        query = lax.broadcasted_iota(jnp.int32, (size, TILE), 1) + (2 * ROWS + half * TILE)
        begin = starts[:, half * TILE : (half + 1) * TILE]

        def body(head, carry):
            cols = columns(half, head)
            raw = dot_nt(window[rows, :HD], qs[cols])
            scores = jnp.where((pos >= begin) & (pos <= query), raw * (FACTOR * LOG2E), NEGATIVE)
            peak = jnp.max(scores, axis=0, keepdims=True)
            weights = jnp.exp2(scores - peak)
            probs[rows, cols] = weights
            near_out[:, cols] = dot(vt[:, rows], weights.astype(BF))
            stats[0:1, cols] = peak
            stats[1:2, cols] = jnp.sum(weights, axis=0, keepdims=True)
            return carry

        lax.fori_loop(0, HEADS, body, 0)

    near_forward(0)
    near_forward(1)
    for copy in second:
        copy.wait_recv()
    kt[:, :ROWS] = window[:ROWS, :HD].T
    vt[:, :ROWS] = window[:ROWS, HD:].T

    def far_part(half):
        rows = slice(half * TILE, ROWS)
        size = rows.stop - rows.start
        pos = lax.broadcasted_iota(jnp.int32, (size, TILE), 0) + rows.start
        begin = starts[:, half * TILE : (half + 1) * TILE]

        def body(head, carry):
            cols = columns(half, head)
            raw = dot_nt(window[rows, :HD], qs[cols])
            scores = jnp.where(pos >= begin, raw * (FACTOR * LOG2E), NEGATIVE)
            near_peak = stats[0:1, cols]
            peak = jnp.maximum(near_peak, jnp.max(scores, axis=0, keepdims=True))
            rescale = jnp.exp2(near_peak - peak)
            weights = jnp.exp2(scores - peak)
            total = stats[1:2, cols] * rescale + jnp.sum(weights, axis=0, keepdims=True)
            inverse = 1.0 / total
            out = near_out[:, cols] * rescale + dot(vt[:, rows], weights.astype(BF))
            out = (out * inverse).astype(BF)
            att_ref[half * TILE : (half + 1) * TILE, pl.ds(pl.multiple_of(head * HD, HD), HD)] = out.T
            delta = jnp.sum(gt[:, cols].astype(F32) * out.astype(F32), axis=0, keepdims=True)
            weights = weights * inverse
            grad = dot_nt(window[rows, HD:], gs[cols])
            low[rows, cols] = weights.astype(BF)
            dscores[rows, cols] = (weights * (grad - delta)).astype(BF)
            stats[2:3, cols] = rescale * inverse
            stats[3:4, cols] = delta
            return carry

        lax.fori_loop(0, HEADS, body, 0)

    far_part(0)
    far_part(1)

    def key_sums(row, cols):
        rows = slice(row, row + SIZE)
        return dot(dscores[rows, cols], qs[cols]) * FACTOR, dot(low[rows, cols], gs[cols])

    back_far = []
    for chunk in range(CHUNKS):
        row = chunk * SIZE
        cols = slice(0, ROWS if row < TILE else COLS)
        dk, dv = key_sums(row, cols)
        part = slice(row, row + SIZE)
        far_out[part, :HD] = dk.astype(BF)
        far_out[part, HD:] = dv.astype(BF)
        copy = send(far_out.at[pl.ds(row, SIZE)], got_far.at[pl.ds(row, SIZE)], f_out.at[chunk], f_in.at[chunk], left)
        copy.start()
        back_far.append(copy)

    def near_back(half, rows):
        def body(head, carry):
            cols = columns(half, head)
            weights = probs[rows, cols] * stats[2:3, cols]
            low[rows, cols] = weights.astype(BF)
            dscores[rows, cols] = (weights * (dprobs[rows, cols] - stats[3:4, cols])).astype(BF)
            return carry

        lax.fori_loop(0, HEADS, body, 0)

    near_back(0, slice(ROWS, 2 * ROWS))
    near_back(1, slice(ROWS, 2 * ROWS))
    back_mid = []
    for chunk in range(CHUNKS):
        row = chunk * SIZE
        part = slice(row, row + SIZE)
        dk, dv = key_sums(ROWS + row, slice(0, COLS))
        back_far[chunk].wait_recv()
        mid_out[part, :HD] = (dk + got_far[part, :HD].astype(F32)).astype(BF)
        mid_out[part, HD:] = (dv + got_far[part, HD:].astype(F32)).astype(BF)
        copy = send(mid_out.at[pl.ds(row, SIZE)], got_mid.at[pl.ds(row, SIZE)], m_out.at[chunk], m_in.at[chunk], left)
        copy.start()
        back_mid.append(copy)

    near_back(0, slice(2 * ROWS, 2 * ROWS + TILE))
    near_back(1, slice(2 * ROWS, 3 * ROWS))
    for chunk in range(CHUNKS):
        row = chunk * SIZE
        part = slice(row, row + SIZE)
        cols = slice(0 if row < TILE else ROWS, COLS)
        dk, dv = key_sums(2 * ROWS + row, cols)
        own_ref[part, :HD] = dk
        own_ref[part, HD:] = dv

    def query_grad(half):
        rows = slice(half * TILE, 2 * ROWS + (half + 1) * TILE)

        def body(head, carry):
            cols = columns(half, head)
            grad = dot(kt[:, rows], dscores[rows, cols]) * FACTOR
            dq_ref[half * TILE : (half + 1) * TILE, pl.ds(pl.multiple_of(head * HD, HD), HD)] = grad.T
            return carry

        lax.fori_loop(0, HEADS, body, 0)

    query_grad(0)
    query_grad(1)
    kvs.sent()
    queries.sent()
    for copy in first + second + back_far + back_mid:
        copy.wait_send()
    for copy in back_mid:
        copy.wait_recv()


def finish_kernel(att, dq, own, got, att_ref, dq_ref, dk_ref, dv_ref, dk, dv, sems):
    copies = [
        pltpu.make_async_copy(src, dst, sems.at[i])
        for i, (src, dst) in enumerate(((att, att_ref), (dq, dq_ref), (dk, dk_ref), (dv, dv_ref)))
    ]
    copies[0].start()
    copies[1].start()
    dk[...] = own[:, :HD] + got[:, :HD].astype(F32)
    copies[2].start()
    dv[...] = own[:, HD:] + got[:, HD:].astype(F32)
    copies[3].start()
    for copy in copies:
        copy.wait()


def specs(space, count):
    return [pl.BlockSpec(memory_space=space)] * count


def shape(*dims, dtype=BF):
    return jax.ShapeDtypeStruct(dims, dtype)


def on_device(queries, keys, values, cotangent, doc_lengths, old_slots):
    dma = pltpu.SemaphoreType.DMA
    bf = lambda *dims: pltpu.VMEM(dims, BF)
    f32 = lambda *dims: pltpu.VMEM(dims, F32)
    slot_bufs = [bf(N, BLK, 2 * HD)] * 2 + [bf(NX, BLK, 2 * HD)]
    out_shape = [
        shape(ROWS, 2 * HD),
        shape(ROWS, 2 * HD, dtype=F32),
        shape(ROWS, 2 * HD, dtype=F32),
        shape(ROWS, 2 * HD),
    ]
    results = pl.pallas_call(
        main_kernel,
        out_shape=out_shape,
        in_specs=specs(pltpu.SMEM, 2) + specs(pltpu.HBM, 4),
        out_specs=specs(pltpu.VMEM, 4),
        scratch_shapes=[bf(PER, BLK, 2 * HD), bf(PER, BLK, HD), bf(PER, BLK, HD), bf(ROWS, 2 * HD)]
        + [pltpu.SMEM((N,), jnp.int32)]
        + slot_bufs * 2
        + [bf(WIN, 2 * HD), bf(HD, WIN), bf(HD, WIN), bf(COLS, HD), bf(COLS, HD), bf(HD, COLS)]
        + [pltpu.VMEM((1, ROWS), jnp.int32)]
        + [f32(WIN, COLS), f32(WIN, COLS), bf(WIN, COLS), bf(WIN, COLS), f32(HD, COLS), f32(8, COLS)]
        + [bf(ROWS, 2 * HD)] * 3
        + [dma((4,))]
        + [dma(())] * 8
        + [dma((CHUNKS,))] * 8,
        compiler_params=pltpu.CompilerParams(
            collective_id=0, has_side_effects=True, vmem_limit_bytes=48 << 20
        ),
        name="exchange_and_attend",
    )(
        old_slots, doc_lengths,
        queries.reshape(PER, BLK, 2 * HD),
        keys.reshape(PER, BLK, HD),
        values.reshape(PER, BLK, HD),
        cotangent,
    )
    return pl.pallas_call(
        finish_kernel,
        out_shape=out_shape[:2] + [shape(ROWS, HD, dtype=F32)] * 2,
        in_specs=specs(pltpu.VMEM, 4),
        out_specs=specs(pltpu.HBM, 4),
        scratch_shapes=[f32(ROWS, HD), f32(ROWS, HD), dma((4,))],
        compiler_params=pltpu.CompilerParams(vmem_limit_bytes=8 << 20),
        name="finish",
    )(*results)


def solution(mesh):
    rows = P(("dp", "ctx"), None)
    return jax.shard_map(
        on_device,
        mesh=mesh,
        in_specs=(rows, rows, rows, rows, P("dp"), P("dp")),
        out_specs=(rows, rows, rows, rows),
        check_vma=False,
    )
```

time: 75.5 us -> 74.3 us (0.984)
  Pallas kernels: 67.5 us -> 69.1 us
  other arithmetic: 1.24 us -> 0 us
  local copies, waits for them, and re-layouts: 5.32 us -> 4.38 us
    pallas_call x3 -> x2, Pallas kernels: 67.5 us -> 69.1 us  [the longest x1 68 us: on_device(): pl.pallas_call(main_kernel, out_shape=out_shape, in_specs=specs(pltpu.SME...]
    select_n x1 -> x0, other arithmetic: 0.8 us -> none  [on_device(): recv_ids = lax.dynamic_slice_in_dim(old_slots, me * PER, PER) // PER]
    reshape x1 -> x0, local copies, waits for them, and re-layouts: 0.76 us -> none  [on_device(): table = old_slots.reshape(N, PER)]
where the time goes in v2:
time: 74.3 us; the launch traced here: 74.1 us
  Pallas kernels  69.1 us (93%)
  local copies, waits for them, and re-layouts  4.38 us (6%)
    pallas_call x1, Pallas kernels, on_device(): pl.pallas_call(main_kernel, out_shape=out_shape, in_specs=specs(pltpu.SME...  68 us
    unnamed x12, local copies, waits for them, and re-layouts  4.38 us

profile of v2, /device:TPU:10, one launch (start us, length us, event | category | flops | bytes accessed | tf_op | source)
XLA Modules:
  0.0 74.1 jit_solution(104533413607003532)
XLA Ops:
  0.6 0.0 copy-start.4
  0.6 0.0 copy-start.5
  0.7 0.7 copy-done.4
  1.3 0.0 copy-done.5
  1.3 0.0 copy-start
  1.3 0.9 %copy-done = bf16[512,256]{1,0:T(8,128)(2,1)S(1)} copy-done((bf16[512,256]{1,0:T(8,128)(2,1)S(1)}, bf16[512,256]{1,0:T(8,128)(2,1)}, u32[]{:S(2)}) %copy-start) | copy-done | bytes 262168
  2.3 0.0 copy-start.1
  2.3 0.9 %copy-done.1 = bf16[512,256]{1,0:T(8,128)(2,1)S(1)} copy-done((bf16[512,256]{1,0:T(8,128)(2,1)S(1)}, bf16[512,256]{1,0:T(8,128)(2,1)}, u32[]{:S(2)}) %copy-start.1) | copy-done | bytes 262168
  3.2 0.0 copy-start.2
  3.2 0.9 %copy-done.2 = bf16[512,128]{1,0:T(8,128)(2,1)S(1)} copy-done((bf16[512,128]{1,0:T(8,128)(2,1)S(1)}, bf16[512,128]{1,0:T(8,128)(2,1)}, u32[]{:S(2)}) %copy-start.2) | copy-done | bytes 131096
  4.1 0.0 copy-start.3
  4.1 0.9 %copy-done.3 = bf16[512,128]{1,0:T(8,128)(2,1)S(1)} copy-done((bf16[512,128]{1,0:T(8,128)(2,1)S(1)}, bf16[512,128]{1,0:T(8,128)(2,1)}, u32[]{:S(2)}) %copy-start.3) | copy-done | bytes 131096
  5.0 68.0 %exchange_and_attend.1 = (bf16[512,256]{1,0:T(8,128)(2,1)S(1)}, f32[512,256]{1,0:T(8,128)S(1)}, f32[512,256]{1,0:T(8,128)S(1)}, bf16[512,256]{1,0:T(8,128)(2,1)S(1)}) custom-call(s32[512]{0:T(512)S(1)} %copy-done.4, s32[64]{0:T(128)S(1)} %copy-done.5, bf16[16,32,256]{2,1,0:T(8,128)(2,1)S(1)} %bitcast.3, bf16[16,32,128]{2,1,0:T(8,128)(2,1)S(1)} %bitcast.4, ...), custom_call_target="tpu_custom_call" | custom-call | tf_op jit(solution)/shard_map/exchange_and_attend/pallas_call | solution.py:419
  73.0 1.1 %finish.1 = (bf16[512,256]{1,0:T(8,128)(2,1)}, f32[512,256]{1,0:T(8,128)}, f32[512,128]{1,0:T(8,128)}, f32[512,128]{1,0:T(8,128)}) custom-call(bf16[512,256]{1,0:T(8,128)(2,1)S(1)} %get-tuple-element.8.att, f32[512,256]{1,0:T(8,128)S(1)} %get-tuple-element.9.dq, f32[512,256]{1,0:T(8,128)S(1)} %get-tuple-element.10.own, ...), custom_call_target="tpu_custom_call" | custom-call | tf_op jit(solution)/shard_map/finish/pallas_call | solution.py:445
Async XLA Ops:
  0.6 0.7 copy-start.4
  0.6 0.7 copy-start.5
  1.3 1.0 %copy-start = (bf16[512,256]{1,0:T(8,128)(2,1)S(1)}, bf16[512,256]{1,0:T(8,128)(2,1)}, u32[]{:S(2)}) copy-start(bf16[512,256]{1,0:T(8,128)(2,1)} %param.6) | copy-start | bytes 786436
  2.3 0.9 %copy-start.1 = (bf16[512,256]{1,0:T(8,128)(2,1)S(1)}, bf16[512,256]{1,0:T(8,128)(2,1)}, u32[]{:S(2)}) copy-start(bf16[512,256]{1,0:T(8,128)(2,1)} %g_hbm.1) | copy-start | bytes 786436
  3.2 0.9 %copy-start.2 = (bf16[512,128]{1,0:T(8,128)(2,1)S(1)}, bf16[512,128]{1,0:T(8,128)(2,1)}, u32[]{:S(2)}) copy-start(bf16[512,128]{1,0:T(8,128)(2,1)} %param.7) | copy-start | bytes 393220
  4.1 0.9 %copy-start.3 = (bf16[512,128]{1,0:T(8,128)(2,1)S(1)}, bf16[512,128]{1,0:T(8,128)(2,1)}, u32[]{:S(2)}) copy-start(bf16[512,128]{1,0:T(8,128)(2,1)} %param.8) | copy-start | bytes 393220

commit v3 on v2

--- a/solution.py
+++ b/solution.py
@@ -99,18 +99,20 @@
     def sent(self):
         part = self.out.at[pl.ds(0, N - 1)]
         pltpu.make_async_copy(part, part, self.out_sem).wait()
+
+    def passed_on(self):
         pltpu.make_async_copy(self.mid, self.mid, self.onward_sem).wait()
 
 
 def main_kernel(
     slots, lengths, q_hbm, k_hbm, v_hbm, g_hbm,
-    att_ref, dq_ref, own_ref, got_mid,
+    att_hbm, dq_hbm, dk_hbm, dv_hbm,
     q_old, k_old, v_old, g_old, held_ids,
     kv_out, kv_into, kv_mid, q_out, q_into, q_mid,
     window, kt, vt, qs, gs, gt, starts,
     probs, dprobs, low, dscores, near_out, stats,
-    far_out, got_far, mid_out,
-    load_sem, kv_out_sem, kv_in_sem, kv_mid_sem, kv_on_sem, q_out_sem, q_in_sem, q_mid_sem, q_on_sem,
+    far_out, got_far, mid_out, got_mid, att, dq, own, dk_all, dv_all,
+    load_sem, store_sem, kv_out_sem, kv_in_sem, kv_mid_sem, kv_on_sem, q_out_sem, q_in_sem, q_mid_sem, q_on_sem,
     h1_out, h1_in, h2_out, h2_in, f_out, f_in, m_out, m_in,
 ):
     me = lax.axis_index("ctx")
@@ -136,7 +138,7 @@
         held = 0
         for j in range(PER):
             slot = slots[dest * PER + j]
-            held = held + jnp.where(slot // PER == me, slot % PER, 0)
+            held = held + jnp.where((slot >> 4) == me, slot & (PER - 1), 0)
         held_ids[dest] = held
         return carry
 
@@ -151,30 +153,30 @@
         return carry
 
     lax.fori_loop(0, N, pack_kv, 0)
-    loads[2].wait()
-
-    def pack_q(dest, carry):
-        q_out[dest] = q_old[held_ids[dest]]
-        return carry
-
-    lax.fori_loop(0, N, pack_q, 0)
     kv_into[me] = kv_out[me]
-    q_into[me] = q_out[me]
     pl.semaphore_wait(barrier, N - 1)
 
     kvs = Exchange(me, kv_out, kv_into, kv_mid, kv_out_sem, kv_in_sem, kv_mid_sem, kv_on_sem)
     queries = Exchange(me, q_out, q_into, q_mid, q_out_sem, q_in_sem, q_mid_sem, q_on_sem)
-    kvs.push_far()
     kvs.push(0)
     for ahead, behind in zip(AHEAD, BEHIND):
         kvs.push(ahead)
         kvs.push(behind)
-    kvs.pass_on()
+    kvs.push(NZ // 2)
+
+    loads[2].wait()
+
+    def pack_q(dest, carry):
+        q_out[dest] = q_old[held_ids[dest]]
+        return carry
+
+    lax.fori_loop(0, N, pack_q, 0)
+    q_into[me] = q_out[me]
     queries.push_far()
     queries.push(0)
-    for behind in BEHIND:
+    for behind, ahead in zip(BEHIND, AHEAD):
         queries.push(behind)
-    queries.pass_on()
+        queries.push(ahead)
 
     loads[3].wait()
     for half in range(2):
@@ -196,7 +198,7 @@
     kvs.received()
 
     def unpack_kv(block, carry):
-        source = slots[me * PER + block] // PER
+        source = slots[me * PER + block] >> 4
         window[pl.ds(pl.multiple_of(2 * ROWS + block * BLK, BLK), BLK)] = kv_into[source]
         return carry
 
@@ -213,8 +215,7 @@
     second = [hop(1, chunk, h2_out, h2_in) for chunk in range(CHUNKS)]
     for copy in first:
         copy.start()
-    for ahead in AHEAD:
-        queries.push(ahead)
+    queries.pass_on()
     for copy, onward in zip(first, second):
         copy.wait_recv()
         onward.start()
@@ -242,7 +243,7 @@
     queries.received()
 
     def unpack_q(block, carry):
-        source = slots[me * PER + block] // PER
+        source = slots[me * PER + block] >> 4
         row = (block // 8) * ROWS + (block % 8) * BLK
         qs[pl.ds(pl.multiple_of(row, BLK), BLK)] = q_into[source, :, :HD]
         qs[pl.ds(pl.multiple_of(row + TILE, BLK), BLK)] = q_into[source, :, HD:]
@@ -273,21 +274,36 @@
 
     near_forward(0)
     near_forward(1)
-    for copy in second:
-        copy.wait_recv()
-    kt[:, :ROWS] = window[:ROWS, :HD].T
-    vt[:, :ROWS] = window[:ROWS, HD:].T
+
+    def far_scores(half, row):
+        rows = slice(row, row + SIZE)
+        pos = lax.broadcasted_iota(jnp.int32, (SIZE, TILE), 0) + row
+        begin = starts[:, half * TILE : (half + 1) * TILE]
+
+        def body(head, carry):
+            cols = columns(half, head)
+            raw = dot_nt(window[rows, :HD], qs[cols])
+            probs[rows, cols] = jnp.where(pos >= begin, raw * (FACTOR * LOG2E), NEGATIVE)
+            dprobs[rows, cols] = dot_nt(window[rows, HD:], gs[cols])
+            return carry
+
+        lax.fori_loop(0, HEADS, body, 0)
+
+    for chunk in range(CHUNKS):
+        second[chunk].wait_recv()
+        row = chunk * SIZE
+        kt[:, row : row + SIZE] = window[row : row + SIZE, :HD].T
+        vt[:, row : row + SIZE] = window[row : row + SIZE, HD:].T
+        far_scores(0, row)
+        if row >= TILE:
+            far_scores(1, row)
 
     def far_part(half):
         rows = slice(half * TILE, ROWS)
-        size = rows.stop - rows.start
-        pos = lax.broadcasted_iota(jnp.int32, (size, TILE), 0) + rows.start
-        begin = starts[:, half * TILE : (half + 1) * TILE]
-
-        def body(head, carry):
-            cols = columns(half, head)
-            raw = dot_nt(window[rows, :HD], qs[cols])
-            scores = jnp.where(pos >= begin, raw * (FACTOR * LOG2E), NEGATIVE)
+
+        def body(head, carry):
+            cols = columns(half, head)
+            scores = probs[rows, cols]
             near_peak = stats[0:1, cols]
             peak = jnp.maximum(near_peak, jnp.max(scores, axis=0, keepdims=True))
             rescale = jnp.exp2(near_peak - peak)
@@ -296,12 +312,11 @@
             inverse = 1.0 / total
             out = near_out[:, cols] * rescale + dot(vt[:, rows], weights.astype(BF))
             out = (out * inverse).astype(BF)
-            att_ref[half * TILE : (half + 1) * TILE, pl.ds(pl.multiple_of(head * HD, HD), HD)] = out.T
+            att[half * TILE : (half + 1) * TILE, pl.ds(pl.multiple_of(head * HD, HD), HD)] = out.T
             delta = jnp.sum(gt[:, cols].astype(F32) * out.astype(F32), axis=0, keepdims=True)
             weights = weights * inverse
-            grad = dot_nt(window[rows, HD:], gs[cols])
             low[rows, cols] = weights.astype(BF)
-            dscores[rows, cols] = (weights * (grad - delta)).astype(BF)
+            dscores[rows, cols] = (weights * (dprobs[rows, cols] - delta)).astype(BF)
             stats[2:3, cols] = rescale * inverse
             stats[3:4, cols] = delta
             return carry
@@ -358,8 +373,8 @@
         part = slice(row, row + SIZE)
         cols = slice(0 if row < TILE else ROWS, COLS)
         dk, dv = key_sums(2 * ROWS + row, cols)
-        own_ref[part, :HD] = dk
-        own_ref[part, HD:] = dv
+        own[part, :HD] = dk
+        own[part, HD:] = dv
 
     def query_grad(half):
         rows = slice(half * TILE, 2 * ROWS + (half + 1) * TILE)
@@ -367,34 +382,49 @@
         def body(head, carry):
             cols = columns(half, head)
             grad = dot(kt[:, rows], dscores[rows, cols]) * FACTOR
-            dq_ref[half * TILE : (half + 1) * TILE, pl.ds(pl.multiple_of(head * HD, HD), HD)] = grad.T
+            dq[half * TILE : (half + 1) * TILE, pl.ds(pl.multiple_of(head * HD, HD), HD)] = grad.T
             return carry
 
         lax.fori_loop(0, HEADS, body, 0)
 
     query_grad(0)
     query_grad(1)
+    stores = [
+        pltpu.make_async_copy(src, dst, store_sem.at[i])
+        for i, (src, dst) in enumerate(((att, att_hbm), (dq, dq_hbm)))
+    ]
+    for store in stores:
+        store.start()
+    for chunk in range(CHUNKS):
+        rows = pl.ds(chunk * SIZE, SIZE)
+        back_mid[chunk].wait_recv()
+        dk_all[rows] = own[rows, :HD] + got_mid[rows, :HD].astype(F32)
+        dv_all[rows] = own[rows, HD:] + got_mid[rows, HD:].astype(F32)
+        for i, (src, dst) in enumerate(((dk_all, dk_hbm), (dv_all, dv_hbm))):
+            store = pltpu.make_async_copy(src.at[rows], dst.at[rows], store_sem.at[2 + 2 * chunk + i])
+            store.start()
+            stores.append(store)
     kvs.sent()
     queries.sent()
+    queries.passed_on()
     for copy in first + second + back_far + back_mid:
         copy.wait_send()
-    for copy in back_mid:
-        copy.wait_recv()
-
-
-def finish_kernel(att, dq, own, got, att_ref, dq_ref, dk_ref, dv_ref, dk, dv, sems):
-    copies = [
-        pltpu.make_async_copy(src, dst, sems.at[i])
-        for i, (src, dst) in enumerate(((att, att_ref), (dq, dq_ref), (dk, dk_ref), (dv, dv_ref)))
-    ]
-    copies[0].start()
-    copies[1].start()
-    dk[...] = own[:, :HD] + got[:, :HD].astype(F32)
-    copies[2].start()
-    dv[...] = own[:, HD:] + got[:, HD:].astype(F32)
-    copies[3].start()
-    for copy in copies:
-        copy.wait()
+    for store in stores:
+        store.wait()
+
+
+def finish_kernel(*refs):
+    results, places, held = refs[:4], refs[4:8], refs[8:12]
+    load_sem, store_sem = refs[12:]
+    loads = [pltpu.make_async_copy(results[i], held[i], load_sem.at[i]) for i in range(4)]
+    stores = [pltpu.make_async_copy(held[i], places[i], store_sem.at[i]) for i in range(4)]
+    for load in loads:
+        load.start()
+    for load, store in zip(loads, stores):
+        load.wait()
+        store.start()
+    for store in stores:
+        store.wait()
 
 
 def specs(space, count):
@@ -413,26 +443,28 @@
     out_shape = [
         shape(ROWS, 2 * HD),
         shape(ROWS, 2 * HD, dtype=F32),
-        shape(ROWS, 2 * HD, dtype=F32),
-        shape(ROWS, 2 * HD),
+        shape(ROWS, HD, dtype=F32),
+        shape(ROWS, HD, dtype=F32),
     ]
     results = pl.pallas_call(
         main_kernel,
         out_shape=out_shape,
         in_specs=specs(pltpu.SMEM, 2) + specs(pltpu.HBM, 4),
-        out_specs=specs(pltpu.VMEM, 4),
+        out_specs=specs(pltpu.HBM, 4),
         scratch_shapes=[bf(PER, BLK, 2 * HD), bf(PER, BLK, HD), bf(PER, BLK, HD), bf(ROWS, 2 * HD)]
         + [pltpu.SMEM((N,), jnp.int32)]
         + slot_bufs * 2
         + [bf(WIN, 2 * HD), bf(HD, WIN), bf(HD, WIN), bf(COLS, HD), bf(COLS, HD), bf(HD, COLS)]
         + [pltpu.VMEM((1, ROWS), jnp.int32)]
         + [f32(WIN, COLS), f32(WIN, COLS), bf(WIN, COLS), bf(WIN, COLS), f32(HD, COLS), f32(8, COLS)]
-        + [bf(ROWS, 2 * HD)] * 3
-        + [dma((4,))]
+        + [bf(ROWS, 2 * HD)] * 5
+        + [f32(ROWS, 2 * HD)] * 2
+        + [f32(ROWS, HD)] * 2
+        + [dma((4,)), dma((2 + 2 * CHUNKS,))]
         + [dma(())] * 8
         + [dma((CHUNKS,))] * 8,
         compiler_params=pltpu.CompilerParams(
-            collective_id=0, has_side_effects=True, vmem_limit_bytes=48 << 20
+            collective_id=0, has_side_effects=True, vmem_limit_bytes=56 << 20
         ),
         name="exchange_and_attend",
     )(
@@ -444,11 +476,12 @@
     )
     return pl.pallas_call(
         finish_kernel,
-        out_shape=out_shape[:2] + [shape(ROWS, HD, dtype=F32)] * 2,
-        in_specs=specs(pltpu.VMEM, 4),
+        out_shape=out_shape,
+        in_specs=specs(pltpu.HBM, 4),
         out_specs=specs(pltpu.HBM, 4),
-        scratch_shapes=[f32(ROWS, HD), f32(ROWS, HD), dma((4,))],
-        compiler_params=pltpu.CompilerParams(vmem_limit_bytes=8 << 20),
+        scratch_shapes=[bf(ROWS, 2 * HD), f32(ROWS, 2 * HD), f32(ROWS, HD), f32(ROWS, HD)]
+        + [dma((4,))] * 2,
+        compiler_params=pltpu.CompilerParams(vmem_limit_bytes=56 << 20),
         name="finish",
     )(*results)
 

time: 74.3 us -> 63.1 us (0.85); the launches traced: 74.1 us -> 62 us
  Pallas kernels: 69.1 us -> 61.4 us
  local copies, waits for them, and re-layouts: 4.38 us -> 0 us
    pallas_call x1, Pallas kernels: 68 us -> 59.2 us  [on_device(): pl.pallas_call(main_kernel, out_shape=out_shape, in_specs=specs(pltpu.SME...]
    unnamed x12 -> x0, local copies, waits for them, and re-layouts: 4.38 us -> none
    pallas_call x1, Pallas kernels: 1.09 us -> 2.15 us  [on_device(): pl.pallas_call(finish_kernel, out_shape=out_shape, in_specs=specs(pltpu.H...]
where the time goes in v3:
time: 63.1 us; the launch traced here: 62 us
  Pallas kernels  61.4 us (97%)
  between operations  0.64 us (1%)
    pallas_call x1, Pallas kernels, on_device(): pl.pallas_call(main_kernel, out_shape=out_shape, in_specs=specs(pltpu.SME...  59.2 us
    pallas_call x1, Pallas kernels, on_device(): pl.pallas_call(finish_kernel, out_shape=out_shape, in_specs=specs(pltpu.H...  2.15 us

profile of v3, /device:TPU:10, one launch (start us, length us, event | category | flops | bytes accessed | tf_op | source)
XLA Modules:
  0.0 62.0 jit_solution(5294917198654118836)
XLA Ops:
  0.6 59.2 %exchange_and_attend.1 = (bf16[512,256]{1,0:T(8,128)(2,1)}, f32[512,256]{1,0:T(8,128)}, f32[512,128]{1,0:T(8,128)}, f32[512,128]{1,0:T(8,128)}) custom-call(s32[512]{0:T(512)} %slots.1, s32[64]{0:T(128)} %lengths.1, bf16[16,32,256]{2,1,0:T(8,128)(2,1)} %bitcast.3, bf16[16,32,128]{2,1,0:T(8,128)(2,1)} %bitcast.4, bf16[16,32,128]{2,1,0:T(8,128)(2,1)} %bitcast.5, ...), custom_call_target="tpu_custom_call" | custom-call | tf_op jit(solution)/shard_map/exchange_and_attend/pallas_call | solution.py:449
  59.9 2.2 %finish.1 = (bf16[512,256]{1,0:T(8,128)(2,1)}, f32[512,256]{1,0:T(8,128)}, f32[512,128]{1,0:T(8,128)}, f32[512,128]{1,0:T(8,128)}) custom-call(bf16[512,256]{1,0:T(8,128)(2,1)} %get-tuple-element.8.refs_0_, f32[512,256]{1,0:T(8,128)} %get-tuple-element.9.refs_1_, f32[512,128]{1,0:T(8,128)} %get-tuple-element.10.refs_2_, f32[512,128]{1,0:T(8,128)} %get-tuple-element.11.refs_3_), custom_call_target="tpu_custom_call" | custom-call | tf_op jit(solution)/shard_map/finish/pallas_call | solution.py:477

commit v4 on v3

--- a/solution.py
+++ b/solution.py
@@ -27,6 +27,7 @@
 F32 = jnp.float32
 BEHIND = (7, 6, 5)
 AHEAD = (1, 2, 3)
+ROUND = 1
 
 
 def peer(index):
@@ -52,7 +53,7 @@
 
 
 class Exchange:
-    def __init__(self, me, out, into, mid, out_sem, in_sem, mid_sem, onward_sem):
+    def __init__(self, me, out, into, out_sem, in_sem, mid=None, mid_sem=None, onward_sem=None):
         self.me = me
         self.out, self.into, self.mid = out, into, mid
         self.out_sem, self.in_sem = out_sem, in_sem
@@ -63,34 +64,40 @@
         z = (self.me % NZ + dz) % NZ
         return x * NZ + z
 
-    def push(self, dz):
+    def push(self, dz, first=0):
         def body(step, carry):
             dest = self.at(near_first(step), dz)
             send(self.out.at[dest], self.into.at[self.me], self.out_sem, self.in_sem, dest).start()
             return carry
 
-        lax.fori_loop(1 if dz == 0 else 0, NX, body, 0)
-
-    def push_far(self):
+        lax.fori_loop(first, NX, body, 0)
+
+    def push_round(self, dz, spot, count):
         def body(step, carry):
             dx = near_first(step)
-            dest = self.at(dx, NZ // 2)
+            dest = self.at(dx, dz)
             way = self.at(dx, NZ - 2)
-            send(self.out.at[dest], self.mid.at[step], self.out_sem, self.mid_sem, way).start()
-            return carry
-
-        lax.fori_loop(0, NX, body, 0)
-
-    def pass_on(self):
+            send(
+                self.out.at[dest], self.mid.at[spot + step], self.out_sem, self.mid_sem, way
+            ).start()
+            return carry
+
+        lax.fori_loop(0, count, body, 0)
+
+    def mid_received(self):
         pltpu.make_async_copy(self.mid, self.mid, self.mid_sem).wait()
-        dest = self.at(0, NZ - 2)
+
+    def pass_on(self, dz, spot, count):
+        dest = self.at(0, dz + 2)
 
         def body(step, carry):
             source = self.at(NX - near_first(step), 2)
-            send(self.mid.at[step], self.into.at[source], self.onward_sem, self.in_sem, dest).start()
-            return carry
-
-        lax.fori_loop(0, NX, body, 0)
+            send(
+                self.mid.at[spot + step], self.into.at[source], self.onward_sem, self.in_sem, dest
+            ).start()
+            return carry
+
+        lax.fori_loop(0, count, body, 0)
 
     def received(self):
         part = self.into.at[pl.ds(0, N - 1)]
@@ -108,11 +115,11 @@
     slots, lengths, q_hbm, k_hbm, v_hbm, g_hbm,
     att_hbm, dq_hbm, dk_hbm, dv_hbm,
     q_old, k_old, v_old, g_old, held_ids,
-    kv_out, kv_into, kv_mid, q_out, q_into, q_mid,
+    kv_out, kv_into, q_out, q_into, q_mid,
     window, kt, vt, qs, gs, gt, starts,
     probs, dprobs, low, dscores, near_out, stats,
     far_out, got_far, mid_out, got_mid, att, dq, own, dk_all, dv_all,
-    load_sem, store_sem, kv_out_sem, kv_in_sem, kv_mid_sem, kv_on_sem, q_out_sem, q_in_sem, q_mid_sem, q_on_sem,
+    load_sem, store_sem, kv_out_sem, kv_in_sem, q_out_sem, q_in_sem, q_mid_sem, q_on_sem,
     h1_out, h1_in, h2_out, h2_in, f_out, f_in, m_out, m_in,
 ):
     me = lax.axis_index("ctx")
@@ -156,9 +163,9 @@
     kv_into[me] = kv_out[me]
     pl.semaphore_wait(barrier, N - 1)
 
-    kvs = Exchange(me, kv_out, kv_into, kv_mid, kv_out_sem, kv_in_sem, kv_mid_sem, kv_on_sem)
-    queries = Exchange(me, q_out, q_into, q_mid, q_out_sem, q_in_sem, q_mid_sem, q_on_sem)
-    kvs.push(0)
+    kvs = Exchange(me, kv_out, kv_into, kv_out_sem, kv_in_sem)
+    queries = Exchange(me, q_out, q_into, q_out_sem, q_in_sem, q_mid, q_mid_sem, q_on_sem)
+    kvs.push(0, 1)
     for ahead, behind in zip(AHEAD, BEHIND):
         kvs.push(ahead)
         kvs.push(behind)
@@ -172,11 +179,12 @@
 
     lax.fori_loop(0, N, pack_q, 0)
     q_into[me] = q_out[me]
-    queries.push_far()
-    queries.push(0)
+    queries.push_round(NZ // 2, 0, NX)
+    queries.push_round(AHEAD[-1], NX, ROUND)
+    queries.push(0, 1)
     for behind, ahead in zip(BEHIND, AHEAD):
         queries.push(behind)
-        queries.push(ahead)
+        queries.push(ahead, ROUND if ahead == AHEAD[-1] else 0)
 
     loads[3].wait()
     for half in range(2):
@@ -215,7 +223,9 @@
     second = [hop(1, chunk, h2_out, h2_in) for chunk in range(CHUNKS)]
     for copy in first:
         copy.start()
-    queries.pass_on()
+    queries.mid_received()
+    queries.pass_on(NZ // 2, 0, NX)
+    queries.pass_on(AHEAD[-1], NX, ROUND)
     for copy, onward in zip(first, second):
         copy.wait_recv()
         onward.start()
@@ -236,7 +246,7 @@
             dprobs[rows, cols] = dot_nt(window[rows, HD:], gs[cols])
             return carry
 
-        lax.fori_loop(0, HEADS, body, 0)
+        lax.fori_loop(0, HEADS, body, 0, unroll=True)
 
     near_dprobs(0)
     near_dprobs(1)
@@ -270,7 +280,7 @@
             stats[1:2, cols] = jnp.sum(weights, axis=0, keepdims=True)
             return carry
 
-        lax.fori_loop(0, HEADS, body, 0)
+        lax.fori_loop(0, HEADS, body, 0, unroll=True)
 
     near_forward(0)
     near_forward(1)
@@ -287,12 +297,11 @@
             dprobs[rows, cols] = dot_nt(window[rows, HD:], gs[cols])
             return carry
 
-        lax.fori_loop(0, HEADS, body, 0)
+        lax.fori_loop(0, HEADS, body, 0, unroll=True)
 
     for chunk in range(CHUNKS):
         second[chunk].wait_recv()
         row = chunk * SIZE
-        kt[:, row : row + SIZE] = window[row : row + SIZE, :HD].T
         vt[:, row : row + SIZE] = window[row : row + SIZE, HD:].T
         far_scores(0, row)
         if row >= TILE:
@@ -321,10 +330,7 @@
             stats[3:4, cols] = delta
             return carry
 
-        lax.fori_loop(0, HEADS, body, 0)
-
-    far_part(0)
-    far_part(1)
+        lax.fori_loop(0, HEADS, body, 0, unroll=True)
 
     def key_sums(row, cols):
         rows = slice(row, row + SIZE)
@@ -333,6 +339,10 @@
     back_far = []
     for chunk in range(CHUNKS):
         row = chunk * SIZE
+        if row == 0:
+            far_part(0)
+        if row == TILE:
+            far_part(1)
         cols = slice(0, ROWS if row < TILE else COLS)
         dk, dv = key_sums(row, cols)
         part = slice(row, row + SIZE)
@@ -342,6 +352,8 @@
         copy.start()
         back_far.append(copy)
 
+    kt[:, :ROWS] = window[:ROWS, :HD].T
+
     def near_back(half, rows):
         def body(head, carry):
             cols = columns(half, head)
@@ -350,7 +362,7 @@
             dscores[rows, cols] = (weights * (dprobs[rows, cols] - stats[3:4, cols])).astype(BF)
             return carry
 
-        lax.fori_loop(0, HEADS, body, 0)
+        lax.fori_loop(0, HEADS, body, 0, unroll=True)
 
     near_back(0, slice(ROWS, 2 * ROWS))
     near_back(1, slice(ROWS, 2 * ROWS))
@@ -385,7 +397,7 @@
             dq[half * TILE : (half + 1) * TILE, pl.ds(pl.multiple_of(head * HD, HD), HD)] = grad.T
             return carry
 
-        lax.fori_loop(0, HEADS, body, 0)
+        lax.fori_loop(0, HEADS, body, 0, unroll=True)
 
     query_grad(0)
     query_grad(1)
@@ -439,7 +451,6 @@
     dma = pltpu.SemaphoreType.DMA
     bf = lambda *dims: pltpu.VMEM(dims, BF)
     f32 = lambda *dims: pltpu.VMEM(dims, F32)
-    slot_bufs = [bf(N, BLK, 2 * HD)] * 2 + [bf(NX, BLK, 2 * HD)]
     out_shape = [
         shape(ROWS, 2 * HD),
         shape(ROWS, 2 * HD, dtype=F32),
@@ -453,7 +464,8 @@
         out_specs=specs(pltpu.HBM, 4),
         scratch_shapes=[bf(PER, BLK, 2 * HD), bf(PER, BLK, HD), bf(PER, BLK, HD), bf(ROWS, 2 * HD)]
         + [pltpu.SMEM((N,), jnp.int32)]
-        + slot_bufs * 2
+        + [bf(N, BLK, 2 * HD)] * 4
+        + [bf(NX + ROUND, BLK, 2 * HD)]
         + [bf(WIN, 2 * HD), bf(HD, WIN), bf(HD, WIN), bf(COLS, HD), bf(COLS, HD), bf(HD, COLS)]
         + [pltpu.VMEM((1, ROWS), jnp.int32)]
         + [f32(WIN, COLS), f32(WIN, COLS), bf(WIN, COLS), bf(WIN, COLS), f32(HD, COLS), f32(8, COLS)]
@@ -461,7 +473,7 @@
         + [f32(ROWS, 2 * HD)] * 2
         + [f32(ROWS, HD)] * 2
         + [dma((4,)), dma((2 + 2 * CHUNKS,))]
-        + [dma(())] * 8
+        + [dma(())] * 6
         + [dma((CHUNKS,))] * 8,
         compiler_params=pltpu.CompilerParams(
             collective_id=0, has_side_effects=True, vmem_limit_bytes=56 << 20

time: 63.1 us -> 59.6 us (0.945)
  Pallas kernels: 61.4 us -> 57.9 us
    pallas_call x1, Pallas kernels: 59.2 us -> 55.7 us  [on_device(): pl.pallas_call(main_kernel, out_shape=out_shape, in_specs=specs(pltpu.SME...]
where the time goes in v4:
time: 59.6 us; the launch traced here: 58.5 us
  Pallas kernels  57.9 us (97%)
  between operations  0.64 us (1%)
    pallas_call x1, Pallas kernels, on_device(): pl.pallas_call(main_kernel, out_shape=out_shape, in_specs=specs(pltpu.SME...  55.7 us
    pallas_call x1, Pallas kernels, on_device(): pl.pallas_call(finish_kernel, out_shape=out_shape, in_specs=specs(pltpu.H...  2.15 us

profile of v4, /device:TPU:10, one launch (start us, length us, event | category | flops | bytes accessed | tf_op | source)
XLA Modules:
  0.0 58.5 jit_solution(4749445214867877360)
XLA Ops:
  0.6 55.7 %exchange_and_attend.1 = (bf16[512,256]{1,0:T(8,128)(2,1)}, f32[512,256]{1,0:T(8,128)}, f32[512,128]{1,0:T(8,128)}, f32[512,128]{1,0:T(8,128)}) custom-call(s32[512]{0:T(512)} %slots.1, s32[64]{0:T(128)} %lengths.1, bf16[16,32,256]{2,1,0:T(8,128)(2,1)} %bitcast.3, bf16[16,32,128]{2,1,0:T(8,128)(2,1)} %bitcast.4, bf16[16,32,128]{2,1,0:T(8,128)(2,1)} %bitcast.5, ...), custom_call_target="tpu_custom_call" | custom-call | tf_op jit(solution)/shard_map/exchange_and_attend/pallas_call | solution.py:460
  56.4 2.2 %finish.1 = (bf16[512,256]{1,0:T(8,128)(2,1)}, f32[512,256]{1,0:T(8,128)}, f32[512,128]{1,0:T(8,128)}, f32[512,128]{1,0:T(8,128)}) custom-call(bf16[512,256]{1,0:T(8,128)(2,1)} %get-tuple-element.8.refs_0_, f32[512,256]{1,0:T(8,128)} %get-tuple-element.9.refs_1_, f32[512,128]{1,0:T(8,128)} %get-tuple-element.10.refs_2_, f32[512,128]{1,0:T(8,128)} %get-tuple-element.11.refs_3_), custom_call_target="tpu_custom_call" | custom-call | tf_op jit(solution)/shard_map/finish/pallas_call | solution.py:489

commit v5 on v4

--- a/solution.py
+++ b/solution.py
@@ -113,12 +113,12 @@
 
 def main_kernel(
     slots, lengths, q_hbm, k_hbm, v_hbm, g_hbm,
-    att_hbm, dq_hbm, dk_hbm, dv_hbm,
+    att_hbm, dq_hbm, own_hbm, got_hbm,
     q_old, k_old, v_old, g_old, held_ids,
     kv_out, kv_into, q_out, q_into, q_mid,
     window, kt, vt, qs, gs, gt, starts,
     probs, dprobs, low, dscores, near_out, stats,
-    far_out, got_far, mid_out, got_mid, att, dq, own, dk_all, dv_all,
+    far_out, got_far, mid_out, att, dq, own,
     load_sem, store_sem, kv_out_sem, kv_in_sem, q_out_sem, q_in_sem, q_mid_sem, q_on_sem,
     h1_out, h1_in, h2_out, h2_in, f_out, f_in, m_out, m_in,
 ):
@@ -304,7 +304,7 @@
         row = chunk * SIZE
         vt[:, row : row + SIZE] = window[row : row + SIZE, HD:].T
         far_scores(0, row)
-        if row >= TILE:
+        if row >= TILE and chunk < CHUNKS - 1:
             far_scores(1, row)
 
     def far_part(half):
@@ -342,6 +342,7 @@
         if row == 0:
             far_part(0)
         if row == TILE:
+            far_scores(1, ROWS - SIZE)
             far_part(1)
         cols = slice(0, ROWS if row < TILE else COLS)
         dk, dv = key_sums(row, cols)
@@ -374,7 +375,7 @@
         back_far[chunk].wait_recv()
         mid_out[part, :HD] = (dk + got_far[part, :HD].astype(F32)).astype(BF)
         mid_out[part, HD:] = (dv + got_far[part, HD:].astype(F32)).astype(BF)
-        copy = send(mid_out.at[pl.ds(row, SIZE)], got_mid.at[pl.ds(row, SIZE)], m_out.at[chunk], m_in.at[chunk], left)
+        copy = send(mid_out.at[pl.ds(row, SIZE)], got_hbm.at[pl.ds(row, SIZE)], m_out.at[chunk], m_in.at[chunk], left)
         copy.start()
         back_mid.append(copy)
 
@@ -403,19 +404,10 @@
     query_grad(1)
     stores = [
         pltpu.make_async_copy(src, dst, store_sem.at[i])
-        for i, (src, dst) in enumerate(((att, att_hbm), (dq, dq_hbm)))
+        for i, (src, dst) in enumerate(((att, att_hbm), (dq, dq_hbm), (own, own_hbm)))
     ]
     for store in stores:
         store.start()
-    for chunk in range(CHUNKS):
-        rows = pl.ds(chunk * SIZE, SIZE)
-        back_mid[chunk].wait_recv()
-        dk_all[rows] = own[rows, :HD] + got_mid[rows, :HD].astype(F32)
-        dv_all[rows] = own[rows, HD:] + got_mid[rows, HD:].astype(F32)
-        for i, (src, dst) in enumerate(((dk_all, dk_hbm), (dv_all, dv_hbm))):
-            store = pltpu.make_async_copy(src.at[rows], dst.at[rows], store_sem.at[2 + 2 * chunk + i])
-            store.start()
-            stores.append(store)
     kvs.sent()
     queries.sent()
     queries.passed_on()
@@ -423,20 +415,45 @@
         copy.wait_send()
     for store in stores:
         store.wait()
-
-
-def finish_kernel(*refs):
-    results, places, held = refs[:4], refs[4:8], refs[8:12]
-    load_sem, store_sem = refs[12:]
-    loads = [pltpu.make_async_copy(results[i], held[i], load_sem.at[i]) for i in range(4)]
-    stores = [pltpu.make_async_copy(held[i], places[i], store_sem.at[i]) for i in range(4)]
-    for load in loads:
-        load.start()
-    for load, store in zip(loads, stores):
-        load.wait()
-        store.start()
-    for store in stores:
-        store.wait()
+    for copy in back_mid:
+        copy.wait_recv()
+
+
+def finish_kernel(
+    att_hbm, dq_hbm, own_hbm, got_hbm, att_ref, dq_ref, dk_ref, dv_ref,
+    att, dq, own, got, dk, dv, load_sem, store_sem,
+):
+    halves = [pl.ds(half * TILE, TILE) for half in range(2)]
+    loads = []
+    for half, rows in enumerate(halves):
+        loads.append([
+            pltpu.make_async_copy(src.at[rows], dst.at[rows], load_sem.at[half, i])
+            for i, (src, dst) in enumerate(
+                ((got_hbm, got), (own_hbm, own), (att_hbm, att), (dq_hbm, dq))
+            )
+        ])
+        for load in loads[half]:
+            load.start()
+    stores = []
+
+    def store(half, i, src, dst):
+        copy = pltpu.make_async_copy(src.at[halves[half]], dst.at[halves[half]], store_sem.at[half, i])
+        copy.start()
+        stores.append(copy)
+
+    for half, rows in enumerate(halves):
+        loads[half][0].wait()
+        loads[half][1].wait()
+        dk[rows] = own[rows, :HD] + got[rows, :HD].astype(F32)
+        store(half, 0, dk, dk_ref)
+        dv[rows] = own[rows, HD:] + got[rows, HD:].astype(F32)
+        store(half, 1, dv, dv_ref)
+        loads[half][2].wait()
+        store(half, 2, att, att_ref)
+        loads[half][3].wait()
+        store(half, 3, dq, dq_ref)
+    for copy in stores:
+        copy.wait()
 
 
 def specs(space, count):
@@ -454,12 +471,10 @@
     out_shape = [
         shape(ROWS, 2 * HD),
         shape(ROWS, 2 * HD, dtype=F32),
-        shape(ROWS, HD, dtype=F32),
-        shape(ROWS, HD, dtype=F32),
     ]
     results = pl.pallas_call(
         main_kernel,
-        out_shape=out_shape,
+        out_shape=out_shape + [shape(ROWS, 2 * HD, dtype=F32), shape(ROWS, 2 * HD)],
         in_specs=specs(pltpu.SMEM, 2) + specs(pltpu.HBM, 4),
         out_specs=specs(pltpu.HBM, 4),
         scratch_shapes=[bf(PER, BLK, 2 * HD), bf(PER, BLK, HD), bf(PER, BLK, HD), bf(ROWS, 2 * HD)]
@@ -469,10 +484,9 @@
         + [bf(WIN, 2 * HD), bf(HD, WIN), bf(HD, WIN), bf(COLS, HD), bf(COLS, HD), bf(HD, COLS)]
         + [pltpu.VMEM((1, ROWS), jnp.int32)]
         + [f32(WIN, COLS), f32(WIN, COLS), bf(WIN, COLS), bf(WIN, COLS), f32(HD, COLS), f32(8, COLS)]
-        + [bf(ROWS, 2 * HD)] * 5
+        + [bf(ROWS, 2 * HD)] * 4
         + [f32(ROWS, 2 * HD)] * 2
-        + [f32(ROWS, HD)] * 2
-        + [dma((4,)), dma((2 + 2 * CHUNKS,))]
+        + [dma((4,)), dma((3,))]
         + [dma(())] * 6
         + [dma((CHUNKS,))] * 8,
         compiler_params=pltpu.CompilerParams(
@@ -488,11 +502,12 @@
     )
     return pl.pallas_call(
         finish_kernel,
-        out_shape=out_shape,
+        out_shape=out_shape + [shape(ROWS, HD, dtype=F32)] * 2,
         in_specs=specs(pltpu.HBM, 4),
         out_specs=specs(pltpu.HBM, 4),
-        scratch_shapes=[bf(ROWS, 2 * HD), f32(ROWS, 2 * HD), f32(ROWS, HD), f32(ROWS, HD)]
-        + [dma((4,))] * 2,
+        scratch_shapes=[bf(ROWS, 2 * HD), f32(ROWS, 2 * HD), f32(ROWS, 2 * HD), bf(ROWS, 2 * HD)]
+        + [f32(ROWS, HD)] * 2
+        + [dma((2, 4))] * 2,
         compiler_params=pltpu.CompilerParams(vmem_limit_bytes=56 << 20),
         name="finish",
     )(*results)

time: 59.6 us -> 59 us (0.990)
  no operation moved by 1% of the time
where the time goes in v5:
time: 59 us; the launch traced here: 58 us
  Pallas kernels  57.4 us (97%)
  between operations  0.64 us (1%)
    pallas_call x1, Pallas kernels, on_device(): pl.pallas_call(main_kernel, out_shape=out_shape + [shape(ROWS, 2 * HD, dt...  55.1 us
    pallas_call x1, Pallas kernels, on_device(): pl.pallas_call(finish_kernel, out_shape=out_shape + [shape(ROWS, HD, dtyp...  2.27 us

profile of v5, /device:TPU:10, one launch (start us, length us, event | category | flops | bytes accessed | tf_op | source)
XLA Modules:
  0.0 58.0 jit_solution(5469697694340486546)
XLA Ops:
  0.6 55.1 %exchange_and_attend.1 = (bf16[512,256]{1,0:T(8,128)(2,1)}, f32[512,256]{1,0:T(8,128)}, f32[512,256]{1,0:T(8,128)}, bf16[512,256]{1,0:T(8,128)(2,1)}) custom-call(s32[512]{0:T(512)} %slots.1, s32[64]{0:T(128)} %lengths.1, bf16[16,32,256]{2,1,0:T(8,128)(2,1)} %bitcast.3, bf16[16,32,128]{2,1,0:T(8,128)(2,1)} %bitcast.4, bf16[16,32,128]{2,1,0:T(8,128)(2,1)} %bitcast.5, ...), custom_call_target="tpu_custom_call" | custom-call | tf_op jit(solution)/shard_map/exchange_and_attend/pallas_call | solution.py:475
  55.7 2.3 %finish.1 = (bf16[512,256]{1,0:T(8,128)(2,1)}, f32[512,256]{1,0:T(8,128)}, f32[512,128]{1,0:T(8,128)}, f32[512,128]{1,0:T(8,128)}) custom-call(bf16[512,256]{1,0:T(8,128)(2,1)} %get-tuple-element.8.att_hbm, f32[512,256]{1,0:T(8,128)} %get-tuple-element.9.dq_hbm, f32[512,256]{1,0:T(8,128)} %get-tuple-element.10.own_hbm, ...), custom_call_target="tpu_custom_call" | custom-call | tf_op jit(solution)/shard_map/finish/pallas_call | solution.py:503

commit v6 on v5

--- a/solution.py
+++ b/solution.py
@@ -210,7 +210,6 @@
         window[pl.ds(pl.multiple_of(2 * ROWS + block * BLK, BLK), BLK)] = kv_into[source]
         return carry
 
-    lax.fori_loop(0, PER, unpack_kv, 0)
 
     def hop(level, chunk, out_sem, in_sem):
         return send(
@@ -221,7 +220,9 @@
 
     first = [hop(0, chunk, h1_out, h1_in) for chunk in range(CHUNKS)]
     second = [hop(1, chunk, h2_out, h2_in) for chunk in range(CHUNKS)]
-    for copy in first:
+    blocks = PER // CHUNKS
+    for chunk, copy in enumerate(first):
+        lax.fori_loop(chunk * blocks, (chunk + 1) * blocks, unpack_kv, 0)
         copy.start()
     queries.mid_received()
     queries.pass_on(NZ // 2, 0, NX)

time: 59 us -> 59 us (level)
  no operation moved by 1% of the time
where the time goes in v6:
time: 59 us; the launch traced here: 58 us
  Pallas kernels  57.4 us (97%)
  between operations  0.64 us (1%)
    pallas_call x1, Pallas kernels, on_device(): pl.pallas_call(main_kernel, out_shape=out_shape + [shape(ROWS, 2 * HD, dt...  55.1 us
    pallas_call x1, Pallas kernels, on_device(): pl.pallas_call(finish_kernel, out_shape=out_shape + [shape(ROWS, HD, dtyp...  2.27 us

profile of v6, /device:TPU:10, one launch (start us, length us, event | category | flops | bytes accessed | tf_op | source)
XLA Modules:
  0.0 58.0 jit_solution(11185606094048114449)
XLA Ops:
  0.6 55.1 %exchange_and_attend.1 = (bf16[512,256]{1,0:T(8,128)(2,1)}, f32[512,256]{1,0:T(8,128)}, f32[512,256]{1,0:T(8,128)}, bf16[512,256]{1,0:T(8,128)(2,1)}) custom-call(s32[512]{0:T(512)} %slots.1, s32[64]{0:T(128)} %lengths.1, bf16[16,32,256]{2,1,0:T(8,128)(2,1)} %bitcast.3, bf16[16,32,128]{2,1,0:T(8,128)(2,1)} %bitcast.4, bf16[16,32,128]{2,1,0:T(8,128)(2,1)} %bitcast.5, ...), custom_call_target="tpu_custom_call" | custom-call | tf_op jit(solution)/shard_map/exchange_and_attend/pallas_call | solution.py:476
  55.7 2.3 %finish.1 = (bf16[512,256]{1,0:T(8,128)(2,1)}, f32[512,256]{1,0:T(8,128)}, f32[512,128]{1,0:T(8,128)}, f32[512,128]{1,0:T(8,128)}) custom-call(bf16[512,256]{1,0:T(8,128)(2,1)} %get-tuple-element.8.att_hbm, f32[512,256]{1,0:T(8,128)} %get-tuple-element.9.dq_hbm, f32[512,256]{1,0:T(8,128)} %get-tuple-element.10.own_hbm, ...), custom_call_target="tpu_custom_call" | custom-call | tf_op jit(solution)/shard_map/finish/pallas_call | solution.py:504
